TPU v7x, 256 devices: a whole 4x4x8 slice. The times are simulated.
256 devices in a mesh: shot: 8 (over y, x_hi), lat: 32 (over z, x_lo, core).
Axes of the slice: x: 4 (x_hi: 2, x_lo: 2; x = x_hi * 2 + x_lo), y: 4, z: 8, core: 2. Of those that a mesh axis runs over, the one named last changes fastest.
Arguments:
- partials: bfloat16 [16, 8, 2048, 2048], P('shot', None, 'lat'), may hold values from -2.5 to 2.5
- wedges: int32 [2048, 2048], P('lat'), may hold values from 0 to 15
- levels: float32 [16], replicated, may hold values from 0.25 to 1.5
Outputs:
- filtered: float32 [8, 2048, 2048], P('shot', 'lat')
All inputs are finite; a program needn't handle non-finite values.
Results may differ from a plain program's by a relative error of at most 0.03.
Values may be sent and summed in bfloat16 or wider, within the bound.
A program may use at most 64 MiB of HBM per device.

v0:
```python
import functools
import math

import jax
import jax.numpy as jnp
import ml_dtypes
import numpy as np
from jax import lax
from jax.experimental import pallas as pl
from jax.experimental.pallas import tpu as pltpu
from jax.sharding import PartitionSpec as P

MESH = pl.DeviceIdType.MESH
F32 = jnp.float32
BF16 = jnp.bfloat16
N = 2048
LAT = 32
ROWS = N // LAT
CHUNKS = 4
CROWS = ROWS // CHUNKS
HALF = math.sqrt(0.5)
NT = (((1,), (1,)), ((), ()))


def owned():
    ky = np.zeros((LAT, 32), np.int64)
    for d in range(LAT):
        for i in range(8):
            for s in (1, 2, 3):
                ky[d, 8 * s + i] = 64 * d + 8 * i + s
        for i in range(4):
            ky[d, i] = 64 * d + 8 * i + 4
        for i in range(4, 7):
            ky[d, i] = 64 * d + 8 * (i - 3)
        ky[d, 7] = 64 * d + (32 if d < 16 else 0)
    return ky


def forward_tables():
    ky = owned()
    y2 = np.arange(256)
    scale = 1.0 / math.sqrt(N)
    parts = []
    for s in range(4):
        rows = ky[:, 8 * s : 8 * s + 8].reshape(-1)
        angle = 2.0 * np.pi * ((rows[:, None] * y2[None, :]) % N) / N
        re, im = np.cos(angle), -np.sin(angle)
        if s == 0:
            packed = 16 * 8 + 7
            re[packed] = 1.0
            im[packed] = np.where(y2 % 2, -1.0, 1.0)
            four = (rows % 8 == 4)[:, None]
            zero = np.zeros_like(re)
            parts += [
                np.where(four, zero, re),
                np.where(four, re, zero),
                np.where(four, zero, im),
                np.where(four, im, zero),
            ]
        else:
            parts += [re, im]
    return (np.concatenate(parts, axis=1) * scale).astype(ml_dtypes.bfloat16)


def inverse_tables():
    ky = owned()
    y2 = np.arange(256)
    scale = 1.0 / math.sqrt(N)
    parts = []
    for s in range(4):
        rows = ky[:, 8 * s : 8 * s + 8].reshape(-1)
        angle = 2.0 * np.pi * ((rows[:, None] * y2[None, :]) % N) / N
        cos, sin = 2.0 * np.cos(angle), 2.0 * np.sin(angle)
        if s == 0:
            packed = 16 * 8 + 7
            cos[packed] = 1.0
            sin[packed] = -np.where(y2 % 2, -1.0, 1.0)
            four = (rows % 8 == 4)[:, None]
            zero = np.zeros_like(cos)
            top = np.concatenate([np.where(four, zero, cos), np.where(four, cos, zero)], axis=1)
            low = np.concatenate([np.where(four, zero, -sin), np.where(four, -sin, zero)], axis=1)
        else:
            top = np.concatenate([cos, sin], axis=1)
            low = np.concatenate([-sin, cos], axis=1)
        parts += [top, low]
    return (np.concatenate(parts, axis=0) * scale).astype(ml_dtypes.bfloat16)


def lateral_tables():
    index = np.arange(128)
    angle = 2.0 * np.pi * ((index[:, None] * index[None, :]) % 128) / 128
    cos, sin = np.cos(angle), np.sin(angle)
    forward = np.block([[cos, -sin], [sin, cos]])
    inverse = np.block([[cos, sin], [-sin, cos]])
    return np.concatenate([forward, inverse], axis=0).astype(ml_dtypes.bfloat16)


def turn_tables():
    angle = 2.0 * np.pi * (np.arange(16)[:, None] * np.arange(128)[None, :]) / N
    scale = 1.0 / math.sqrt(N)
    cos, sin = np.cos(angle) * scale, np.sin(angle) * scale
    return np.stack([cos, -sin, 0.5 * cos, 0.5 * sin]).astype(np.float32)


def pick_tables():
    own = np.zeros((48, 64))
    mirror = np.zeros((48, 64))
    for i in range(8):
        for s in (1, 2, 3):
            own[8 * s + i, 8 * i + s] = 1
            mirror[8 * s + i, 8 * (7 - i) + 8 - s] = 1
    for i in range(4):
        own[i, 8 * i + 4] = 1
        mirror[i, 8 * (7 - i) + 4] = 1
    for i in range(4, 7):
        own[i, 8 * (i - 3)] = 1
        mirror[i, 8 * (11 - i)] = 1
    own[7, 32] = mirror[7, 32] = 1
    own[39, 0] = mirror[39, 0] = 1
    return np.concatenate([own, mirror], axis=0).astype(ml_dtypes.bfloat16)


def lane_tables():
    lanes = np.arange(128)
    place = (lanes % 16) * 8 + lanes // 16
    own = np.zeros((128, 128))
    own[lanes, place] = 1
    mirror = np.zeros((256, 128))
    mirror[128 - lanes, place] = 1
    return np.concatenate([own, mirror], axis=0).astype(ml_dtypes.bfloat16)


def turn(pair, step, length, sign):
    re, im = pair
    step = step % length
    if step == 0:
        return pair
    if 4 * step == length:
        return (-im, re) if sign > 0 else (im, -re)
    if 8 * step == length:
        return ((re - sign * im) * HALF, (im + sign * re) * HALF)
    if 8 * step == 3 * length:
        return ((-re - sign * im) * HALF, (-im + sign * re) * HALF)
    cos = math.cos(2.0 * math.pi * step / length)
    sin = sign * math.sin(2.0 * math.pi * step / length)
    return (re * cos - im * sin, im * cos + re * sin)


def short_transform(values, sign):
    count = len(values)
    if count == 1:
        return values
    even = short_transform(values[0::2], sign)
    odd = short_transform(values[1::2], sign)
    low, high = [], []
    for k in range(count // 2):
        re, im = turn(odd[k], k, count, sign)
        low.append((even[k][0] + re, even[k][1] + im))
        high.append((even[k][0] - re, even[k][1] - im))
    return low + high


def real_eight(u):
    a = [u[k] + u[k + 4] for k in range(4)]
    b = [u[k] - u[k + 4] for k in range(4)]
    even, odd = a[0] + a[2], a[1] + a[3]
    minus, plus = (b[1] - b[3]) * HALF, (b[1] + b[3]) * HALF
    return (
        even + odd,
        even - odd,
        (b[0] + minus, -(b[2] + plus)),
        (a[0] - a[2], a[3] - a[1]),
        (b[0] - minus, b[2] - plus),
    )


def real_eight_back(zero, four, one, two, three):
    plus, minus = zero + four, zero - four
    (r1, i1), (r2, i2), (r3, i3) = one, two, three
    p0, p1 = plus + r2, plus - r2
    m0, m1 = minus - i2, minus + i2
    e0, e1 = r1 + r3, i3 - i1
    o0 = (r1 - i1 - r3 - i3) * HALF
    o1 = (r3 - i3 - r1 - i1) * HALF
    return [p0 + e0, m0 + o0, p1 + e1, m1 + o1, p0 - e0, m0 - o0, p1 - e1, m1 - o1]


def spread(tiles, lane):
    for bit in (8, 4, 2, 1):
        high = (lane // 8) % (2 * bit) >= bit
        new = list(tiles)
        for t in range(16):
            if t & bit:
                continue
            first, second = tiles[t], tiles[t | bit]
            new[t] = jnp.where(high, pltpu.roll(second, 8 * bit, 1), first)
            new[t | bit] = jnp.where(high, second, pltpu.roll(first, 128 - 8 * bit, 1))
        tiles = new
    return tiles


def kernel(
    part_hbm, wedge_hbm, levels, ft_hbm, it_hbm, xt_hbm, tw_hbm, pick_hbm, lane_hbm,
    out,
    part, wedge, ft, it, xt, tw, pick, lanet,
    relay, side, final, cross,
    folded0, folded1, send, held, xr, xi, level1, level2, own_ids, mir_ids, spec_ids, mir_in, spec_in, back, got, mid,
    load_sem, table_sem, relay_s, relay_r, side_s, side_r, final_s, final_r, cross_s, cross_r,
    first_s, first_r, second_s, second_r, wedge_s, wedge_r,
):
    shot = lax.axis_index("shot")
    lat = lax.axis_index("lat")
    n_shot = lax.axis_size("shot")
    y, xh = shot // 2, shot % 2
    up, down = (shot + 2) % n_shot, (shot + n_shot - 2) % n_shot
    y_up, y_down, y_far = (y + 1) % 4, (y + 3) % 4, (y + 2) % 4
    flip = lat + 2 - 4 * ((lat // 2) % 2)
    other = shot + 1 - 2 * xh

    def rows(c):
        return pl.ds(c * CROWS, CROWS)

    loads = [
        pltpu.make_async_copy(
            part_hbm.at[:, :, rows(c), :], part.at[:, :, rows(c), :], load_sem.at[c]
        )
        for c in range(CHUNKS)
    ]
    loads[0].start()
    tables = [
        pltpu.make_async_copy(src, dst, table_sem.at[k])
        for k, (src, dst) in enumerate(
            [(wedge_hbm, wedge), (pick_hbm, pick), (lane_hbm, lanet), (ft_hbm, ft),
             (xt_hbm, xt), (tw_hbm, tw), (it_hbm, it)]
        )
    ]
    for c in range(1, CHUNKS):
        loads[c].start()
    for copy in tables:
        copy.start()

    barrier = pltpu.get_barrier_semaphore()

    def greet(s, l):
        pl.semaphore_signal(barrier, inc=1, device_id=(s, l), device_id_type=MESH)

    @pl.loop(1, LAT)
    def _(k):
        greet(shot, (lat + k) % LAT)

    greet(up, lat)
    greet(down, lat)
    greet(other, flip)
    pl.semaphore_wait(barrier, LAT - 1 + 3)

    def copy_to(src, dst, s_sem, r_sem, s, l):
        return pltpu.make_async_remote_copy(
            src_ref=src, dst_ref=dst, send_sem=s_sem, recv_sem=r_sem, device_id=(s, l), device_id_type=MESH
        )

    def slab(q, c):
        return part.at[0, q, rows(c), :]

    def relay_copy(c, k):
        q = 2 * y_far + k
        return copy_to(
            slab(q, c), relay.at[c, k], relay_s.at[c, k], relay_r.at[c, k], up if k == 0 else down, lat
        )

    def side_copy(c, k):
        q = 2 * y_up + 1 if k == 0 else 2 * y_down
        return copy_to(
            slab(q, c), side.at[c, k], side_s.at[c, k], side_r.at[c, k], up if k == 0 else down, lat
        )

    def final_copy(c, k):
        q = 2 * y_up if k == 0 else 2 * y_down + 1
        return copy_to(
            slab(q, c), final.at[c, k], final_s.at[c, k], final_r.at[c, k], up if k == 0 else down, lat
        )

    def cross_copy(c, h):
        return copy_to(
            slab(2 * y + h, c), cross.at[c, xh], cross_s.at[c, h], cross_r.at[c, xh], 2 * y + h, flip
        )

    def pair(q, c):
        return part[0, q, rows(c), :].astype(F32) + part[1, q, rows(c), :].astype(F32)

    def begin(c):
        loads[c].wait()
        for k in range(2):
            q = 2 * y_far + k
            part[0, q, rows(c), :] = pair(q, c).astype(BF16)
            relay_copy(c, k).start()
        for k in range(2):
            q = 2 * y_up + 1 if k == 0 else 2 * y_down
            part[0, q, rows(c), :] = pair(q, c).astype(BF16)
            side_copy(c, k).start()

    def forward(c):
        for k in range(2):
            q = 2 * y_up if k == 0 else 2 * y_down + 1
            relay_copy(c, k).wait_recv()
            part[0, q, rows(c), :] = (pair(q, c) + relay[c, k].astype(F32)).astype(BF16)
            final_copy(c, k).start()

    def across(c):
        for k in range(2):
            side_copy(c, k).wait_recv()
            final_copy(c, k).wait_recv()
        for h in range(2):
            q = 2 * y + h
            total = pair(q, c) + final[c, h].astype(F32) + side[c, 1 - h].astype(F32)
            part[0, q, rows(c), :] = total.astype(BF16)
            cross_copy(c, h).start()

    def fold(c):
        for h in range(2):
            pltpu.make_async_copy(cross.at[c, h], cross.at[c, h], cross_r.at[c, h]).wait()
        top, low = pl.ds(c * CROWS, CROWS), pl.ds(ROWS + c * CROWS, CROWS)
        u = []
        for k in range(8):
            cols = pl.ds(256 * k, 256)
            u.append(cross[c, 0, :, cols].astype(F32) + cross[c, 1, :, cols].astype(F32))
        zero, four, one, two, three = real_eight(u)
        zero, four = zero.astype(BF16), four.astype(BF16)
        blank = jnp.zeros((CROWS, 512), BF16)
        folded0[top, 0:256] = zero
        folded0[top, 256:512] = four
        folded0[top, 512:1024] = blank
        folded0[low, 0:512] = blank
        folded0[low, 512:768] = zero
        folded0[low, 768:1024] = four
        for s, (re, im) in enumerate((one, two, three)):
            re, im, neg = re.astype(BF16), im.astype(BF16), (-im).astype(BF16)
            folded1[s, top, 0:256] = re
            folded1[s, top, 256:512] = neg
            folded1[s, low, 0:256] = im
            folded1[s, low, 256:512] = re

    lane = lax.broadcasted_iota(jnp.int32, (1, 128), 1)
    seventh = lax.broadcasted_iota(jnp.int32, (8, 128), 0) == 7

    partner = LAT - 1 - lat
    corner = jnp.where(lat == 0, 16, LAT - lat)

    def mirror_copy():
        return copy_to(
            mir_ids.at[:, pl.ds(0, 32), :], mir_in, wedge_s.at[0], wedge_r.at[0], shot, partner
        )

    def corner_copy(k):
        src = (own_ids if k == 0 else mir_ids).at[:, pl.ds(32, 16), :]
        return copy_to(src, spec_in.at[k], wedge_s.at[1 + k], wedge_r.at[1 + k], shot, corner)

    def wedges_out():
        for k in range(3):
            tables[k].wait()
        ids = wedge[...].astype(F32).astype(BF16)
        chosen = jnp.dot(pick[...], ids, preferred_element_type=F32).astype(BF16)
        own, mir = chosen[:48], chosen[48:]
        tall = jnp.concatenate([own[:, 128 * t : 128 * t + 128] for t in range(16)], axis=0)
        moved = jnp.dot(tall, lanet[0:128, :], preferred_element_type=F32)
        for t, tile in enumerate(spread([moved[48 * t : 48 * t + 48] for t in range(16)], lane)):
            own_ids[t] = tile.astype(BF16)
        tall = jnp.concatenate(
            [
                jnp.concatenate(
                    [mir[:, 128 * (15 - t) : 128 * (16 - t)],
                     mir[:, 128 * ((16 - t) % 16) : 128 * ((16 - t) % 16) + 128]],
                    axis=1,
                )
                for t in range(16)
            ],
            axis=0,
        )
        moved = jnp.dot(tall, lanet[128:384, :], preferred_element_type=F32)
        for t, tile in enumerate(spread([moved[48 * t : 48 * t + 48] for t in range(16)], lane)):
            mir_ids[t] = tile.astype(BF16)
        mirror_copy().start()

        @pl.when(lat < 16)
        def _():
            for k in range(2):
                corner_copy(k).start()

    def look_up(ids):
        found = jnp.full(ids.shape, levels[0], F32)
        for w in range(1, 16):
            found = jnp.where(ids == float(w), levels[w], found)
        return found

    def wedges_in():
        mirror_copy().wait_recv()

        @pl.when(lat >= 16)
        def _():
            for k in range(2):
                corner_copy(k).wait_recv()

        @pl.loop(0, 16)
        def _(kk):
            own = own_ids[kk].astype(F32)
            mir = mir_ids[kk].astype(F32)
            got_mir = mir_in[kk].astype(F32)
            spec_own = spec_in[0, kk].astype(F32)
            spec_mir = spec_in[1, kk].astype(F32)
            level1[kk, 0:8, :] = look_up(jnp.where(seventh & (lat >= 16), own[32:40], own[0:8]))
            level1[kk, 8:32, :] = look_up(own[8:32])
            level1[kk, 32:40, :] = look_up(spec_own[0:8])
            row = jnp.where(lat == 16, mir[32:40], spec_mir[0:8])
            level2[kk, 0:8, :] = look_up(jnp.where(seventh & (lat >= 16), row, got_mir[0:8]))
            level2[kk, 8:32, :] = look_up(got_mir[8:32])
            level2[kk, 32:40, :] = look_up(spec_mir[0:8])

    begin(0)
    begin(1)
    forward(0)
    wedges_out()
    begin(2)
    forward(1)
    across(0)
    begin(3)
    forward(2)
    across(1)
    fold(0)
    forward(3)
    across(2)
    fold(1)
    wedges_in()
    across(3)
    fold(2)
    for k in range(3, 7):
        tables[k].wait()
    fold(3)

    pieces = [
        lax.dot_general(ft[:, 0:1024], folded0[...], NT, preferred_element_type=F32).reshape(LAT, 8, 128)
    ]
    for s in range(3):
        pieces.append(
            lax.dot_general(
                ft[:, 1024 + 512 * s : 1536 + 512 * s], folded1[s], NT, preferred_element_type=F32
            ).reshape(LAT, 8, 128)
        )
    for k in range(2):
        both = jnp.concatenate([pieces[2 * k], pieces[2 * k + 1]], axis=1)
        send[:, 16 * k : 16 * k + 16, :] = both.astype(BF16)

    def first_copy(dest):
        return copy_to(send.at[dest], held.at[flip], first_s, first_r, shot, dest)

    @pl.loop(1, LAT)
    def _(k):
        first_copy((lat + k) % LAT).start()

    held[flip] = send[lat]
    all_but_one = held.at[pl.ds(0, LAT - 1)]
    pltpu.make_async_copy(all_but_one, all_but_one, first_r).wait()

    low = lane < 64
    packed = seventh & (lat == 16)
    nothing = jnp.zeros((8, 128), F32)
    for p in range(16):
        u0, u1 = held[2 * p].astype(F32), held[2 * p + 1].astype(F32)
        re = jnp.where(low, u0, pltpu.roll(u1, 64, 1))
        im = jnp.where(low, pltpu.roll(u0, 64, 1), u1)
        xr[p, 0:32, :] = re
        xi[p, 0:8, :] = jnp.where(packed, 0.0, im[0:8])
        xi[p, 8:32, :] = im[8:32]
        xr[p, 32:40, :] = im[0:8]
        xi[p, 32:40, :] = nothing

    def lateral(sign):
        base = 0 if sign < 0 else 2

        @pl.loop(0, 5)
        def _(g):
            at = pl.ds(pl.multiple_of(8 * g, 8), 8)
            values = []
            for p in range(16):
                value = (xr[p, at, :], xi[p, at, :])
                if sign > 0:
                    cos, sin = tw[base, p : p + 1, :], tw[base + 1, p : p + 1, :]
                    value = (value[0] * cos - value[1] * sin, value[1] * cos + value[0] * sin)
                values.append(value)
            for p, value in enumerate(short_transform(values, sign)):
                if sign < 0:
                    cos, sin = tw[base, p : p + 1, :], tw[base + 1, p : p + 1, :]
                    value = (value[0] * cos - value[1] * sin, value[1] * cos + value[0] * sin)
                xr[p, at, :] = value[0]
                xi[p, at, :] = value[1]

    lateral(-1)
    for b in range(4):
        some = pl.ds(4 * b, 4)
        both = jnp.concatenate([xr[some].reshape(160, 128), xi[some].reshape(160, 128)], axis=1)
        spectrum = jnp.dot(both.astype(BF16), xt[0:256, :], preferred_element_type=F32)
        re, im = spectrum[:, :128], spectrum[:, 128:]
        inverse = lax.rsqrt(jnp.maximum(re * re + im * im, 1e-30))
        factor = jnp.maximum(1.0 - level1[some].reshape(160, 128) * inverse, 0.0)
        factor += jnp.maximum(1.0 - level2[some].reshape(160, 128) * inverse, 0.0)
        both = jnp.concatenate([re * factor, im * factor], axis=1)
        inner = jnp.dot(both.astype(BF16), xt[256:512, :], preferred_element_type=F32)
        xr[some] = inner[:, :128].reshape(4, 40, 128)
        xi[some] = inner[:, 128:].reshape(4, 40, 128)
    lateral(1)

    for p in range(16):
        re, im = xr[p, 0:32, :], xi[p, 0:32, :]
        im = jnp.concatenate([jnp.where(packed, xr[p, 32:40, :], im[0:8]), im[8:32]], axis=0)
        back[2 * p] = jnp.where(low, re, pltpu.roll(im, 64, 1)).astype(BF16)
        back[2 * p + 1] = jnp.where(low, pltpu.roll(re, 64, 1), im).astype(BF16)

    def second_copy(dest):
        return copy_to(back.at[dest], got.at[lat], second_s, second_r, shot, dest)

    @pl.loop(1, LAT)
    def _(k):
        second_copy((lat + k) % LAT).start()

    got[lat] = back[lat]
    all_but_one = got.at[pl.ds(0, LAT - 1)]
    pltpu.make_async_copy(all_but_one, all_but_one, second_r).wait()

    for s in range(4):
        tall = got[:, 16 * (s // 2) : 16 * (s // 2) + 16, :].astype(F32)
        flat = tall[:, 8 * (s % 2) : 8 * (s % 2) + 8, :].reshape(256, 128).T.astype(BF16)
        wide = jnp.concatenate([flat[:64], flat[64:]], axis=1)
        mid[s] = jnp.dot(wide, it[512 * s : 512 * s + 512, :], preferred_element_type=F32)

    @pl.loop(0, 8)
    def _(g):
        at = pl.ds(pl.multiple_of(8 * g, 8), 8)
        parts = [(mid[s, at, 0:256], mid[s, at, 256:512]) for s in range(4)]
        values = real_eight_back(parts[0][0], parts[0][1], parts[1], parts[2], parts[3])
        for k in range(8):
            out[0, at, 256 * k : 256 * k + 256] = values[k]

    for c in range(CHUNKS):
        for k in range(2):
            relay_copy(c, k).wait_send()
            side_copy(c, k).wait_send()
            final_copy(c, k).wait_send()
            cross_copy(c, k).wait_send()
    sent = send.at[pl.ds(0, LAT - 1)]
    pltpu.make_async_copy(sent, sent, first_s).wait()
    sent = back.at[pl.ds(0, LAT - 1)]
    pltpu.make_async_copy(sent, sent, second_s).wait()
    mirror_copy().wait_send()

    @pl.when(lat < 16)
    def _():
        for k in range(2):
            corner_copy(k).wait_send()


def on_device(partials, wedges, levels):
    tables = [
        jnp.asarray(t)
        for t in (
            forward_tables(), inverse_tables(), lateral_tables(), turn_tables(), pick_tables(), lane_tables()
        )
    ]
    anywhere = pl.BlockSpec(memory_space=pl.ANY)
    vmem, dma = pltpu.VMEM, pltpu.SemaphoreType.DMA
    two = dma((CHUNKS, 2))
    return pl.pallas_call(
        kernel,
        out_shape=jax.ShapeDtypeStruct((1, ROWS, N), F32),
        in_specs=[anywhere, anywhere, pl.BlockSpec(memory_space=pltpu.SMEM)] + [anywhere] * 6,
        out_specs=pl.BlockSpec(memory_space=pltpu.VMEM),
        scratch_shapes=[
            vmem(partials.shape, BF16),
            vmem(wedges.shape, jnp.int32),
            *[vmem(t.shape, t.dtype) for t in tables],
            vmem((CHUNKS, 2, CROWS, N), BF16),
            vmem((CHUNKS, 2, CROWS, N), BF16),
            vmem((CHUNKS, 2, CROWS, N), BF16),
            vmem((CHUNKS, 2, CROWS, N), BF16),
            vmem((128, 1024), BF16),
            vmem((3, 128, 512), BF16),
            vmem((LAT, 32, 128), BF16),
            vmem((LAT, 32, 128), BF16),
            vmem((16, 40, 128), F32),
            vmem((16, 40, 128), F32),
            vmem((16, 40, 128), F32),
            vmem((16, 40, 128), F32),
            vmem((16, 48, 128), BF16),
            vmem((16, 48, 128), BF16),
            vmem((16, 16, 128), BF16),
            vmem((16, 32, 128), BF16),
            vmem((2, 16, 16, 128), BF16),
            vmem((LAT, 32, 128), BF16),
            vmem((LAT, 32, 128), BF16),
            vmem((4, ROWS, 512), F32),
            dma((CHUNKS,)),
            dma((7,)),
            two, two, two, two, two, two, two, two,
            dma, dma, dma, dma,
            dma((3,)),
            dma((3,)),
        ],
        compiler_params=pltpu.CompilerParams(
            collective_id=0, has_side_effects=True, vmem_limit_bytes=40 * 1024 * 1024
        ),
        name="stack_threshold",
    )(partials, wedges, levels, *tables)


def solution(mesh):
    in_specs = (P("shot", None, "lat", None), P("lat", None), P())
    return jax.shard_map(
        on_device, mesh=mesh, in_specs=in_specs, out_specs=P("shot", "lat", None), check_vma=False
    )
```

profile of v0, /device:TPU:1, one launch (start us, length us, event | category | flops | bytes accessed | tf_op | source)
XLA Modules:
  0.0 69.2 jit_solution(4861094855109993326)
XLA Ops:
  0.0 0.0 copy-start
  0.0 2.2 %copy-done = bf16[2,8,64,2048]{3,2,1,0:T(8,128)(2,1)S(1)} copy-done((bf16[2,8,64,2048]{3,2,1,0:T(8,128)(2,1)S(1)}, bf16[2,8,64,2048]{3,2,1,0:T(8,128)(2,1)}, u32[]{:S(2)}) %copy-start) | copy-done | bytes 4194328
  2.2 0.0 copy-start.1
  2.2 1.6 %copy-done.1 = bf16[2048,512]{1,0:T(8,128)(2,1)S(1)} copy-done((bf16[2048,512]{1,0:T(8,128)(2,1)S(1)}, bf16[2048,512]{1,0:T(8,128)(2,1)}, u32[]{:S(2)}) %copy-start.1) | copy-done | bytes 2097176
  3.8 0.0 copy-start.2
  3.8 1.3 %copy-done.2 = bf16[256,2560]{1,0:T(8,128)(2,1)S(1)} copy-done((bf16[256,2560]{1,0:T(8,128)(2,1)S(1)}, bf16[256,2560]{1,0:T(8,128)(2,1)}, u32[]{:S(2)}) %copy-start.2) | copy-done | bytes 1310744
  5.1 0.0 copy-start.3
  5.1 1.0 %copy-done.3 = s32[64,2048]{1,0:T(8,128)S(1)} copy-done((s32[64,2048]{1,0:T(8,128)S(1)}, s32[64,2048]{1,0:T(8,128)}, u32[]{:S(2)}) %copy-start.3) | copy-done | bytes 524312
  6.1 0.0 copy-start.4
  6.1 0.9 %copy-done.4 = bf16[512,256]{1,0:T(8,128)(2,1)S(1)} copy-done((bf16[512,256]{1,0:T(8,128)(2,1)S(1)}, bf16[512,256]{1,0:T(8,128)(2,1)}, u32[]{:S(2)}) %copy-start.4) | copy-done | bytes 262168
  7.1 0.0 copy-start.5
  7.1 0.9 %copy-done.5 = bf16[384,128]{1,0:T(8,128)(2,1)S(1)} copy-done((bf16[384,128]{1,0:T(8,128)(2,1)S(1)}, bf16[384,128]{1,0:T(8,128)(2,1)}, u32[]{:S(2)}) %copy-start.5) | copy-done | bytes 98328
  8.0 0.0 copy-start.6
  8.0 0.8 %copy-done.6 = f32[4,16,128]{2,1,0:T(8,128)S(1)} copy-done((f32[4,16,128]{2,1,0:T(8,128)S(1)}, f32[4,16,128]{2,1,0:T(8,128)}, u32[]{:S(2)}) %copy-start.6) | copy-done | bytes 32792
  8.7 0.0 copy-start.7
  8.7 0.7 %copy-done.7 = bf16[96,64]{1,0:T(8,128)(2,1)S(1)} copy-done((bf16[96,64]{1,0:T(8,128)(2,1)S(1)}, bf16[96,64]{1,0:T(8,128)(2,1)}, u32[]{:S(2)}) %copy-start.7) | copy-done | bytes 12312
  9.5 0.0 copy-start.8
  9.5 0.7 copy-done.8
  10.1 58.3 %stack_threshold.1 = f32[1,64,2048]{2,1,0:T(8,128)S(1)} custom-call(bf16[2,8,64,2048]{3,2,1,0:T(8,128)(2,1)S(1)} %copy-done, s32[64,2048]{1,0:T(8,128)S(1)} %copy-done.3, f32[16]{0:T(128)S(1)} %copy-done.8, bf16[256,2560]{1,0:T(8,128)(2,1)S(1)} %copy-done.2, bf16[2048,512]{1,0:T(8,128)(2,1)S(1)} %copy-done.1, bf16[512,256]{1,0:T(8,128)(2,1)S(1)} %copy-done.4, ...), custom_call_target="tpu_custom_call" | custom-call | tf_op jit(solution)/shard_map/stack_threshold/pallas_call | solution.py:569
  68.4 0.8 %copy.11 = f32[1,64,2048]{2,1,0:T(8,128)} copy(f32[1,64,2048]{2,1,0:T(8,128)S(1)} %stack_threshold.1) | data formatting | bytes 1048576
Async XLA Ops:
  0.0 2.2 %copy-start = (bf16[2,8,64,2048]{3,2,1,0:T(8,128)(2,1)S(1)}, bf16[2,8,64,2048]{3,2,1,0:T(8,128)(2,1)}, u32[]{:S(2)}) copy-start(bf16[2,8,64,2048]{3,2,1,0:T(8,128)(2,1)} %part_hbm.1) | copy-start | bytes 12582916
  2.2 1.6 %copy-start.1 = (bf16[2048,512]{1,0:T(8,128)(2,1)S(1)}, bf16[2048,512]{1,0:T(8,128)(2,1)}, u32[]{:S(2)}) copy-start(bf16[2048,512]{1,0:T(8,128)(2,1)} %constant.13.clone.it_hbm) | copy-start | bytes 6291460
  3.8 1.3 %copy-start.2 = (bf16[256,2560]{1,0:T(8,128)(2,1)S(1)}, bf16[256,2560]{1,0:T(8,128)(2,1)}, u32[]{:S(2)}) copy-start(bf16[256,2560]{1,0:T(8,128)(2,1)} %constant.12.clone.ft_hbm) | copy-start | bytes 3932164
  5.1 1.0 %copy-start.3 = (s32[64,2048]{1,0:T(8,128)S(1)}, s32[64,2048]{1,0:T(8,128)}, u32[]{:S(2)}) copy-start(s32[64,2048]{1,0:T(8,128)} %wedge_hbm.1) | copy-start | bytes 1572868
  6.1 0.9 %copy-start.4 = (bf16[512,256]{1,0:T(8,128)(2,1)S(1)}, bf16[512,256]{1,0:T(8,128)(2,1)}, u32[]{:S(2)}) copy-start(bf16[512,256]{1,0:T(8,128)(2,1)} %constant.14.clone.xt_hbm) | copy-start | bytes 786436
  7.1 0.9 %copy-start.5 = (bf16[384,128]{1,0:T(8,128)(2,1)S(1)}, bf16[384,128]{1,0:T(8,128)(2,1)}, u32[]{:S(2)}) copy-start(bf16[384,128]{1,0:T(8,128)(2,1)} %constant.17.clone.lane_hbm) | copy-start | bytes 294916
  8.0 0.8 %copy-start.6 = (f32[4,16,128]{2,1,0:T(8,128)S(1)}, f32[4,16,128]{2,1,0:T(8,128)}, u32[]{:S(2)}) copy-start(f32[4,16,128]{2,1,0:T(8,128)} %constant.15.clone.tw_hbm) | copy-start | bytes 98308
  8.7 0.7 %copy-start.7 = (bf16[96,64]{1,0:T(8,128)(2,1)S(1)}, bf16[96,64]{1,0:T(8,128)(2,1)}, u32[]{:S(2)}) copy-start(bf16[96,64]{1,0:T(8,128)(2,1)} %constant.16.clone.pick_hbm) | copy-start | bytes 36868
  9.5 0.7 copy-start.8
where the time goes:
time: 69.7 us; the launch traced here: 69.2 us
  Pallas kernels  58.3 us (84%)
  local copies, waits for them, and re-layouts  10.9 us (16%)
    pallas_call x1, Pallas kernels, on_device(): pl.pallas_call(kernel, out_shape=jax.ShapeDtypeStruct((1, ROWS, N), F32),...  58.3 us
    unnamed x19, local copies, waits for them, and re-layouts  10.9 us

commit v1 on v0

--- a/solution.py
+++ b/solution.py
@@ -47,8 +47,8 @@
         re, im = np.cos(angle), -np.sin(angle)
         if s == 0:
             packed = 16 * 8 + 7
-            re[packed] = 1.0
-            im[packed] = np.where(y2 % 2, -1.0, 1.0)
+            re[packed] = np.where(y2 % 2, -1.0, 1.0)
+            im[packed] = 1.0
             four = (rows % 8 == 4)[:, None]
             zero = np.zeros_like(re)
             parts += [
@@ -73,8 +73,8 @@
         cos, sin = 2.0 * np.cos(angle), 2.0 * np.sin(angle)
         if s == 0:
             packed = 16 * 8 + 7
-            cos[packed] = 1.0
-            sin[packed] = -np.where(y2 % 2, -1.0, 1.0)
+            cos[packed] = np.where(y2 % 2, -1.0, 1.0)
+            sin[packed] = -1.0
             four = (rows % 8 == 4)[:, None]
             zero = np.zeros_like(cos)
             top = np.concatenate([np.where(four, zero, cos), np.where(four, cos, zero)], axis=1)
@@ -204,7 +204,7 @@
     out,
     part, wedge, ft, it, xt, tw, pick, lanet,
     relay, side, final, cross,
-    folded0, folded1, send, held, xr, xi, level1, level2, own_ids, mir_ids, spec_ids, mir_in, spec_in, back, got, mid,
+    folded0, folded1, send, held, xr, xi, level1, level2, own_ids, mir_ids, mir_in, spec_in, back, got, mid,
     load_sem, table_sem, relay_s, relay_r, side_s, side_r, final_s, final_r, cross_s, cross_r,
     first_s, first_r, second_s, second_r, wedge_s, wedge_r,
 ):
@@ -563,7 +563,7 @@
             forward_tables(), inverse_tables(), lateral_tables(), turn_tables(), pick_tables(), lane_tables()
         )
     ]
-    anywhere = pl.BlockSpec(memory_space=pl.ANY)
+    anywhere = pl.BlockSpec(memory_space=pltpu.HBM)
     vmem, dma = pltpu.VMEM, pltpu.SemaphoreType.DMA
     two = dma((CHUNKS, 2))
     return pl.pallas_call(
@@ -589,7 +589,6 @@
             vmem((16, 40, 128), F32),
             vmem((16, 48, 128), BF16),
             vmem((16, 48, 128), BF16),
-            vmem((16, 16, 128), BF16),
             vmem((16, 32, 128), BF16),
             vmem((2, 16, 16, 128), BF16),
             vmem((LAT, 32, 128), BF16),
@@ -603,7 +602,7 @@
             dma((3,)),
         ],
         compiler_params=pltpu.CompilerParams(
-            collective_id=0, has_side_effects=True, vmem_limit_bytes=40 * 1024 * 1024
+            collective_id=0, has_side_effects=True, vmem_limit_bytes=60 * 1024 * 1024
         ),
         name="stack_threshold",
     )(partials, wedges, levels, *tables)

time: 69.7 us -> 60.5 us (0.87)
  local copies, waits for them, and re-layouts: 10.9 us -> 1.87 us
    unnamed x19 -> x1, local copies, waits for them, and re-layouts: 10.9 us -> 1.87 us
where the time goes in v1:
time: 60.5 us; the launch traced here: 60.3 us
  Pallas kernels  58.5 us (97%)
  local copies, waits for them, and re-layouts  1.87 us (3%)
    pallas_call x1, Pallas kernels, on_device(): pl.pallas_call(kernel, out_shape=jax.ShapeDtypeStruct((1, ROWS, N), F32),...  58.5 us
    unnamed x1, local copies, waits for them, and re-layouts  1.87 us

profile of v1, /device:TPU:1, one launch (start us, length us, event | category | flops | bytes accessed | tf_op | source)
XLA Modules:
  0.0 60.3 jit_solution(10804816760618405187)
XLA Ops:
  0.0 58.5 %stack_threshold.1 = f32[1,64,2048]{2,1,0:T(8,128)} custom-call(bf16[2,8,64,2048]{3,2,1,0:T(8,128)(2,1)} %part_hbm.1, s32[64,2048]{1,0:T(8,128)} %wedge_hbm.1, f32[16]{0:T(128)} %levels.1, bf16[256,2560]{1,0:T(8,128)(2,1)} %constant.12.clone.ft_hbm, bf16[2048,512]{1,0:T(8,128)(2,1)} %constant.13.clone.it_hbm, bf16[512,256]{1,0:T(8,128)(2,1)} %constant.14.clone.xt_hbm, ...), custom_call_target="tpu_custom_call" | custom-call | tf_op jit(solution)/shard_map/stack_threshold/pallas_call | solution.py:569
  58.5 1.9 %copy.11 = f32[1,64,2048]{2,1,0:T(8,128)} copy(f32[1,64,2048]{2,1,0:T(8,128)} %stack_threshold.1) | data formatting | bytes 1048576

commit v2 on v1

--- a/solution.py
+++ b/solution.py
@@ -206,7 +206,7 @@
     relay, side, final, cross,
     folded0, folded1, send, held, xr, xi, level1, level2, own_ids, mir_ids, mir_in, spec_in, back, got, mid,
     load_sem, table_sem, relay_s, relay_r, side_s, side_r, final_s, final_r, cross_s, cross_r,
-    first_s, first_r, second_s, second_r, wedge_s, wedge_r,
+    first_s, first_r, second_s, second_r, wedge_s, wedge_r, met,
 ):
     shot = lax.axis_index("shot")
     lat = lax.axis_index("lat")
@@ -244,14 +244,23 @@
     def greet(s, l):
         pl.semaphore_signal(barrier, inc=1, device_id=(s, l), device_id_type=MESH)
 
-    @pl.loop(1, LAT)
-    def _(k):
-        greet(shot, (lat + k) % LAT)
-
+    def neighbour(bit):
+        return lat + bit - 2 * bit * ((lat // bit) % 2)
+
+    bits = (1, 2, 4, 8, 16)
+    for bit in bits:
+        greet(shot, neighbour(bit))
     greet(up, lat)
     greet(down, lat)
     greet(other, flip)
-    pl.semaphore_wait(barrier, LAT - 1 + 3)
+
+    def meet(k):
+        if k > 0:
+            pl.semaphore_wait(met.at[k - 1], 1)
+        if k < len(bits):
+            pl.semaphore_signal(
+                met.at[k], inc=1, device_id=(shot, neighbour(bits[k])), device_id_type=MESH
+            )
 
     def copy_to(src, dst, s_sem, r_sem, s, l):
         return pltpu.make_async_remote_copy(
@@ -287,16 +296,20 @@
     def pair(q, c):
         return part[0, q, rows(c), :].astype(F32) + part[1, q, rows(c), :].astype(F32)
 
-    def begin(c):
+    def prepare(c):
         loads[c].wait()
+        for q in (2 * y_far, 2 * y_far + 1, 2 * y_up + 1, 2 * y_down):
+            part[0, q, rows(c), :] = pair(q, c).astype(BF16)
+
+    def launch(c):
         for k in range(2):
-            q = 2 * y_far + k
-            part[0, q, rows(c), :] = pair(q, c).astype(BF16)
             relay_copy(c, k).start()
         for k in range(2):
-            q = 2 * y_up + 1 if k == 0 else 2 * y_down
-            part[0, q, rows(c), :] = pair(q, c).astype(BF16)
             side_copy(c, k).start()
+
+    def begin(c):
+        prepare(c)
+        launch(c)
 
     def forward(c):
         for k in range(2):
@@ -339,7 +352,15 @@
             folded1[s, low, 0:256] = im
             folded1[s, low, 256:512] = re
 
+    def first_copy(dest):
+        return copy_to(send.at[dest], held.at[flip], first_s, first_r, shot, dest)
+
+    def second_copy(dest):
+        return copy_to(back.at[dest], got.at[lat], second_s, second_r, shot, dest)
+
     lane = lax.broadcasted_iota(jnp.int32, (1, 128), 1)
+    low = lane < 64
+    packed = (lax.broadcasted_iota(jnp.int32, (8, 128), 0) == 7) & (lat == 16)
     seventh = lax.broadcasted_iota(jnp.int32, (8, 128), 0) == 7
 
     partner = LAT - 1 - lat
@@ -378,6 +399,8 @@
         moved = jnp.dot(tall, lanet[128:384, :], preferred_element_type=F32)
         for t, tile in enumerate(spread([moved[48 * t : 48 * t + 48] for t in range(16)], lane)):
             mir_ids[t] = tile.astype(BF16)
+
+    def wedges_go():
         mirror_copy().start()
 
         @pl.when(lat < 16)
@@ -414,63 +437,70 @@
             level2[kk, 8:32, :] = look_up(got_mir[8:32])
             level2[kk, 32:40, :] = look_up(spec_mir[0:8])
 
-    begin(0)
-    begin(1)
-    forward(0)
-    wedges_out()
-    begin(2)
-    forward(1)
-    across(0)
-    begin(3)
-    forward(2)
-    across(1)
-    fold(0)
-    forward(3)
-    across(2)
-    fold(1)
-    wedges_in()
-    across(3)
-    fold(2)
-    for k in range(3, 7):
-        tables[k].wait()
-    fold(3)
-
-    pieces = [
-        lax.dot_general(ft[:, 0:1024], folded0[...], NT, preferred_element_type=F32).reshape(LAT, 8, 128)
-    ]
-    for s in range(3):
-        pieces.append(
-            lax.dot_general(
-                ft[:, 1024 + 512 * s : 1536 + 512 * s], folded1[s], NT, preferred_element_type=F32
-            ).reshape(LAT, 8, 128)
-        )
-    for k in range(2):
-        both = jnp.concatenate([pieces[2 * k], pieces[2 * k + 1]], axis=1)
-        send[:, 16 * k : 16 * k + 16, :] = both.astype(BF16)
-
-    def first_copy(dest):
-        return copy_to(send.at[dest], held.at[flip], first_s, first_r, shot, dest)
-
-    @pl.loop(1, LAT)
-    def _(k):
-        first_copy((lat + k) % LAT).start()
-
-    held[flip] = send[lat]
-    all_but_one = held.at[pl.ds(0, LAT - 1)]
-    pltpu.make_async_copy(all_but_one, all_but_one, first_r).wait()
-
-    low = lane < 64
-    packed = seventh & (lat == 16)
-    nothing = jnp.zeros((8, 128), F32)
-    for p in range(16):
-        u0, u1 = held[2 * p].astype(F32), held[2 * p + 1].astype(F32)
-        re = jnp.where(low, u0, pltpu.roll(u1, 64, 1))
-        im = jnp.where(low, pltpu.roll(u0, 64, 1), u1)
-        xr[p, 0:32, :] = re
-        xi[p, 0:8, :] = jnp.where(packed, 0.0, im[0:8])
-        xi[p, 8:32, :] = im[8:32]
-        xr[p, 32:40, :] = im[0:8]
-        xi[p, 32:40, :] = nothing
+    def stack():
+        prepare(0)
+        pl.semaphore_wait(barrier, len(bits) + 3)
+        launch(0)
+        meet(0)
+        begin(1)
+        meet(1)
+        forward(0)
+        meet(2)
+        wedges_out()
+        meet(3)
+        begin(2)
+        forward(1)
+        meet(4)
+        across(0)
+        begin(3)
+        meet(5)
+        wedges_go()
+        forward(2)
+        across(1)
+        fold(0)
+        forward(3)
+        across(2)
+        fold(1)
+        wedges_in()
+        across(3)
+        fold(2)
+        for k in range(3, 7):
+            tables[k].wait()
+        fold(3)
+
+    def columns():
+        pieces = [
+            lax.dot_general(ft[:, 0:1024], folded0[...], NT, preferred_element_type=F32).reshape(LAT, 8, 128)
+        ]
+        for s in range(3):
+            pieces.append(
+                lax.dot_general(
+                    ft[:, 1024 + 512 * s : 1536 + 512 * s], folded1[s], NT, preferred_element_type=F32
+                ).reshape(LAT, 8, 128)
+            )
+        for k in range(2):
+            both = jnp.concatenate([pieces[2 * k], pieces[2 * k + 1]], axis=1)
+            send[:, 16 * k : 16 * k + 16, :] = both.astype(BF16)
+
+        @pl.loop(1, LAT)
+        def _(k):
+            first_copy((lat + k) % LAT).start()
+
+        held[flip] = send[lat]
+        all_but_one = held.at[pl.ds(0, LAT - 1)]
+        pltpu.make_async_copy(all_but_one, all_but_one, first_r).wait()
+
+    def unpack():
+        nothing = jnp.zeros((8, 128), F32)
+        for p in range(16):
+            u0, u1 = held[2 * p].astype(F32), held[2 * p + 1].astype(F32)
+            re = jnp.where(low, u0, pltpu.roll(u1, 64, 1))
+            im = jnp.where(low, pltpu.roll(u0, 64, 1), u1)
+            xr[p, 0:32, :] = re
+            xi[p, 0:8, :] = jnp.where(packed, 0.0, im[0:8])
+            xi[p, 8:32, :] = im[8:32]
+            xr[p, 32:40, :] = im[0:8]
+            xi[p, 32:40, :] = nothing
 
     def lateral(sign):
         base = 0 if sign < 0 else 2
@@ -492,68 +522,78 @@
                 xr[p, at, :] = value[0]
                 xi[p, at, :] = value[1]
 
-    lateral(-1)
-    for b in range(4):
-        some = pl.ds(4 * b, 4)
-        both = jnp.concatenate([xr[some].reshape(160, 128), xi[some].reshape(160, 128)], axis=1)
-        spectrum = jnp.dot(both.astype(BF16), xt[0:256, :], preferred_element_type=F32)
-        re, im = spectrum[:, :128], spectrum[:, 128:]
-        inverse = lax.rsqrt(jnp.maximum(re * re + im * im, 1e-30))
-        factor = jnp.maximum(1.0 - level1[some].reshape(160, 128) * inverse, 0.0)
-        factor += jnp.maximum(1.0 - level2[some].reshape(160, 128) * inverse, 0.0)
-        both = jnp.concatenate([re * factor, im * factor], axis=1)
-        inner = jnp.dot(both.astype(BF16), xt[256:512, :], preferred_element_type=F32)
-        xr[some] = inner[:, :128].reshape(4, 40, 128)
-        xi[some] = inner[:, 128:].reshape(4, 40, 128)
-    lateral(1)
-
-    for p in range(16):
-        re, im = xr[p, 0:32, :], xi[p, 0:32, :]
-        im = jnp.concatenate([jnp.where(packed, xr[p, 32:40, :], im[0:8]), im[8:32]], axis=0)
-        back[2 * p] = jnp.where(low, re, pltpu.roll(im, 64, 1)).astype(BF16)
-        back[2 * p + 1] = jnp.where(low, pltpu.roll(re, 64, 1), im).astype(BF16)
-
-    def second_copy(dest):
-        return copy_to(back.at[dest], got.at[lat], second_s, second_r, shot, dest)
-
-    @pl.loop(1, LAT)
-    def _(k):
-        second_copy((lat + k) % LAT).start()
-
-    got[lat] = back[lat]
-    all_but_one = got.at[pl.ds(0, LAT - 1)]
-    pltpu.make_async_copy(all_but_one, all_but_one, second_r).wait()
-
-    for s in range(4):
-        tall = got[:, 16 * (s // 2) : 16 * (s // 2) + 16, :].astype(F32)
-        flat = tall[:, 8 * (s % 2) : 8 * (s % 2) + 8, :].reshape(256, 128).T.astype(BF16)
-        wide = jnp.concatenate([flat[:64], flat[64:]], axis=1)
-        mid[s] = jnp.dot(wide, it[512 * s : 512 * s + 512, :], preferred_element_type=F32)
-
-    @pl.loop(0, 8)
-    def _(g):
-        at = pl.ds(pl.multiple_of(8 * g, 8), 8)
-        parts = [(mid[s, at, 0:256], mid[s, at, 256:512]) for s in range(4)]
-        values = real_eight_back(parts[0][0], parts[0][1], parts[1], parts[2], parts[3])
-        for k in range(8):
-            out[0, at, 256 * k : 256 * k + 256] = values[k]
-
-    for c in range(CHUNKS):
-        for k in range(2):
-            relay_copy(c, k).wait_send()
-            side_copy(c, k).wait_send()
-            final_copy(c, k).wait_send()
-            cross_copy(c, k).wait_send()
-    sent = send.at[pl.ds(0, LAT - 1)]
-    pltpu.make_async_copy(sent, sent, first_s).wait()
-    sent = back.at[pl.ds(0, LAT - 1)]
-    pltpu.make_async_copy(sent, sent, second_s).wait()
-    mirror_copy().wait_send()
-
-    @pl.when(lat < 16)
-    def _():
-        for k in range(2):
-            corner_copy(k).wait_send()
+    def middle():
+        lateral(-1)
+        for b in range(4):
+            some = pl.ds(4 * b, 4)
+            both = jnp.concatenate([xr[some].reshape(160, 128), xi[some].reshape(160, 128)], axis=1)
+            spectrum = jnp.dot(both.astype(BF16), xt[0:256, :], preferred_element_type=F32)
+            re, im = spectrum[:, :128], spectrum[:, 128:]
+            inverse = lax.rsqrt(jnp.maximum(re * re + im * im, 1e-30))
+            factor = jnp.maximum(1.0 - level1[some].reshape(160, 128) * inverse, 0.0)
+            factor += jnp.maximum(1.0 - level2[some].reshape(160, 128) * inverse, 0.0)
+            both = jnp.concatenate([re * factor, im * factor], axis=1)
+            inner = jnp.dot(both.astype(BF16), xt[256:512, :], preferred_element_type=F32)
+            xr[some] = inner[:, :128].reshape(4, 40, 128)
+            xi[some] = inner[:, 128:].reshape(4, 40, 128)
+        lateral(1)
+
+    def turn_back():
+        for p in range(16):
+            re, im = xr[p, 0:32, :], xi[p, 0:32, :]
+            im = jnp.concatenate([jnp.where(packed, xr[p, 32:40, :], im[0:8]), im[8:32]], axis=0)
+            back[2 * p] = jnp.where(low, re, pltpu.roll(im, 64, 1)).astype(BF16)
+            back[2 * p + 1] = jnp.where(low, pltpu.roll(re, 64, 1), im).astype(BF16)
+
+        @pl.loop(1, LAT)
+        def _(k):
+            second_copy((lat + k) % LAT).start()
+
+        got[lat] = back[lat]
+        all_but_one = got.at[pl.ds(0, LAT - 1)]
+        pltpu.make_async_copy(all_but_one, all_but_one, second_r).wait()
+
+    def columns_back():
+        for s in range(4):
+            tall = got[:, 16 * (s // 2) : 16 * (s // 2) + 16, :].astype(F32)
+            flat = tall[:, 8 * (s % 2) : 8 * (s % 2) + 8, :].reshape(256, 128).T.astype(BF16)
+            wide = jnp.concatenate([flat[:64], flat[64:]], axis=1)
+            mid[s] = jnp.dot(wide, it[512 * s : 512 * s + 512, :], preferred_element_type=F32)
+
+        @pl.loop(0, 8)
+        def _(g):
+            at = pl.ds(pl.multiple_of(8 * g, 8), 8)
+            parts = [(mid[s, at, 0:256], mid[s, at, 256:512]) for s in range(4)]
+            values = real_eight_back(parts[0][0], parts[0][1], parts[1], parts[2], parts[3])
+            for k in range(8):
+                out[0, at, 256 * k : 256 * k + 256] = values[k]
+
+    def drain():
+        for c in range(CHUNKS):
+            for k in range(2):
+                relay_copy(c, k).wait_send()
+                side_copy(c, k).wait_send()
+                final_copy(c, k).wait_send()
+                cross_copy(c, k).wait_send()
+        sent = send.at[pl.ds(0, LAT - 1)]
+        pltpu.make_async_copy(sent, sent, first_s).wait()
+        sent = back.at[pl.ds(0, LAT - 1)]
+        pltpu.make_async_copy(sent, sent, second_s).wait()
+        mirror_copy().wait_send()
+
+        @pl.when(lat < 16)
+        def _():
+            for k in range(2):
+                corner_copy(k).wait_send()
+
+
+    stack()
+    columns()
+    unpack()
+    middle()
+    turn_back()
+    columns_back()
+    drain()
 
 
 def on_device(partials, wedges, levels):
@@ -600,9 +640,10 @@
             dma, dma, dma, dma,
             dma((3,)),
             dma((3,)),
+            pltpu.SemaphoreType.REGULAR((5,)),
         ],
         compiler_params=pltpu.CompilerParams(
-            collective_id=0, has_side_effects=True, vmem_limit_bytes=60 * 1024 * 1024
+            collective_id=0, has_side_effects=True, vmem_limit_bytes=32 * 1024 * 1024
         ),
         name="stack_threshold",
     )(partials, wedges, levels, *tables)

time: 60.5 us -> 67.4 us (1.11)
  local copies, waits for them, and re-layouts: 1.87 us -> 10.9 us
  Pallas kernels: 58.5 us -> 56 us
    unnamed x1 -> x19, local copies, waits for them, and re-layouts: 1.87 us -> 10.9 us
    pallas_call x1, Pallas kernels: 58.5 us -> 56 us  [on_device(): pl.pallas_call(kernel, out_shape=jax.ShapeDtypeStruct((1, ROWS, N), F32),...]
where the time goes in v2:
time: 67.4 us; the launch traced here: 67 us
  Pallas kernels  56 us (83%)
  local copies, waits for them, and re-layouts  10.9 us (16%)
    pallas_call x1, Pallas kernels, on_device(): pl.pallas_call(kernel, out_shape=jax.ShapeDtypeStruct((1, ROWS, N), F32),...  56 us
    unnamed x19, local copies, waits for them, and re-layouts  10.9 us

profile of v2, /device:TPU:1, one launch (start us, length us, event | category | flops | bytes accessed | tf_op | source)
XLA Modules:
  0.0 67.0 jit_solution(7083773318696020927)
XLA Ops:
  0.0 0.0 copy-start
  0.0 2.2 %copy-done = bf16[2,8,64,2048]{3,2,1,0:T(8,128)(2,1)S(1)} copy-done((bf16[2,8,64,2048]{3,2,1,0:T(8,128)(2,1)S(1)}, bf16[2,8,64,2048]{3,2,1,0:T(8,128)(2,1)}, u32[]{:S(2)}) %copy-start) | copy-done | bytes 4194328
  2.2 0.0 copy-start.1
  2.2 1.6 %copy-done.1 = bf16[2048,512]{1,0:T(8,128)(2,1)S(1)} copy-done((bf16[2048,512]{1,0:T(8,128)(2,1)S(1)}, bf16[2048,512]{1,0:T(8,128)(2,1)}, u32[]{:S(2)}) %copy-start.1) | copy-done | bytes 2097176
  3.8 0.0 copy-start.2
  3.8 1.3 %copy-done.2 = bf16[256,2560]{1,0:T(8,128)(2,1)S(1)} copy-done((bf16[256,2560]{1,0:T(8,128)(2,1)S(1)}, bf16[256,2560]{1,0:T(8,128)(2,1)}, u32[]{:S(2)}) %copy-start.2) | copy-done | bytes 1310744
  5.1 0.0 copy-start.3
  5.1 1.0 %copy-done.3 = s32[64,2048]{1,0:T(8,128)S(1)} copy-done((s32[64,2048]{1,0:T(8,128)S(1)}, s32[64,2048]{1,0:T(8,128)}, u32[]{:S(2)}) %copy-start.3) | copy-done | bytes 524312
  6.1 0.0 copy-start.4
  6.1 0.9 %copy-done.4 = bf16[512,256]{1,0:T(8,128)(2,1)S(1)} copy-done((bf16[512,256]{1,0:T(8,128)(2,1)S(1)}, bf16[512,256]{1,0:T(8,128)(2,1)}, u32[]{:S(2)}) %copy-start.4) | copy-done | bytes 262168
  7.1 0.0 copy-start.5
  7.1 0.9 %copy-done.5 = bf16[384,128]{1,0:T(8,128)(2,1)S(1)} copy-done((bf16[384,128]{1,0:T(8,128)(2,1)S(1)}, bf16[384,128]{1,0:T(8,128)(2,1)}, u32[]{:S(2)}) %copy-start.5) | copy-done | bytes 98328
  8.0 0.0 copy-start.6
  8.0 0.8 %copy-done.6 = f32[4,16,128]{2,1,0:T(8,128)S(1)} copy-done((f32[4,16,128]{2,1,0:T(8,128)S(1)}, f32[4,16,128]{2,1,0:T(8,128)}, u32[]{:S(2)}) %copy-start.6) | copy-done | bytes 32792
  8.7 0.0 copy-start.7
  8.7 0.7 %copy-done.7 = bf16[96,64]{1,0:T(8,128)(2,1)S(1)} copy-done((bf16[96,64]{1,0:T(8,128)(2,1)S(1)}, bf16[96,64]{1,0:T(8,128)(2,1)}, u32[]{:S(2)}) %copy-start.7) | copy-done | bytes 12312
  9.5 0.0 copy-start.8
  9.5 0.7 copy-done.8
  10.1 56.0 %stack_threshold.1 = f32[1,64,2048]{2,1,0:T(8,128)S(1)} custom-call(bf16[2,8,64,2048]{3,2,1,0:T(8,128)(2,1)S(1)} %copy-done, s32[64,2048]{1,0:T(8,128)S(1)} %copy-done.3, f32[16]{0:T(128)S(1)} %copy-done.8, bf16[256,2560]{1,0:T(8,128)(2,1)S(1)} %copy-done.2, bf16[2048,512]{1,0:T(8,128)(2,1)S(1)} %copy-done.1, bf16[512,256]{1,0:T(8,128)(2,1)S(1)} %copy-done.4, ...), custom_call_target="tpu_custom_call" | custom-call | tf_op jit(solution)/shard_map/stack_threshold/pallas_call | solution.py:609
  66.2 0.8 %copy.11 = f32[1,64,2048]{2,1,0:T(8,128)} copy(f32[1,64,2048]{2,1,0:T(8,128)S(1)} %stack_threshold.1) | data formatting | bytes 1048576
Async XLA Ops:
  0.0 2.2 %copy-start = (bf16[2,8,64,2048]{3,2,1,0:T(8,128)(2,1)S(1)}, bf16[2,8,64,2048]{3,2,1,0:T(8,128)(2,1)}, u32[]{:S(2)}) copy-start(bf16[2,8,64,2048]{3,2,1,0:T(8,128)(2,1)} %part_hbm.1) | copy-start | bytes 12582916
  2.2 1.6 %copy-start.1 = (bf16[2048,512]{1,0:T(8,128)(2,1)S(1)}, bf16[2048,512]{1,0:T(8,128)(2,1)}, u32[]{:S(2)}) copy-start(bf16[2048,512]{1,0:T(8,128)(2,1)} %constant.13.clone.it_hbm) | copy-start | bytes 6291460
  3.8 1.3 %copy-start.2 = (bf16[256,2560]{1,0:T(8,128)(2,1)S(1)}, bf16[256,2560]{1,0:T(8,128)(2,1)}, u32[]{:S(2)}) copy-start(bf16[256,2560]{1,0:T(8,128)(2,1)} %constant.12.clone.ft_hbm) | copy-start | bytes 3932164
  5.1 1.0 %copy-start.3 = (s32[64,2048]{1,0:T(8,128)S(1)}, s32[64,2048]{1,0:T(8,128)}, u32[]{:S(2)}) copy-start(s32[64,2048]{1,0:T(8,128)} %wedge_hbm.1) | copy-start | bytes 1572868
  6.1 0.9 %copy-start.4 = (bf16[512,256]{1,0:T(8,128)(2,1)S(1)}, bf16[512,256]{1,0:T(8,128)(2,1)}, u32[]{:S(2)}) copy-start(bf16[512,256]{1,0:T(8,128)(2,1)} %constant.14.clone.xt_hbm) | copy-start | bytes 786436
  7.1 0.9 %copy-start.5 = (bf16[384,128]{1,0:T(8,128)(2,1)S(1)}, bf16[384,128]{1,0:T(8,128)(2,1)}, u32[]{:S(2)}) copy-start(bf16[384,128]{1,0:T(8,128)(2,1)} %constant.17.clone.lane_hbm) | copy-start | bytes 294916
  8.0 0.8 %copy-start.6 = (f32[4,16,128]{2,1,0:T(8,128)S(1)}, f32[4,16,128]{2,1,0:T(8,128)}, u32[]{:S(2)}) copy-start(f32[4,16,128]{2,1,0:T(8,128)} %constant.15.clone.tw_hbm) | copy-start | bytes 98308
  8.7 0.7 %copy-start.7 = (bf16[96,64]{1,0:T(8,128)(2,1)S(1)}, bf16[96,64]{1,0:T(8,128)(2,1)}, u32[]{:S(2)}) copy-start(bf16[96,64]{1,0:T(8,128)(2,1)} %constant.16.clone.pick_hbm) | copy-start | bytes 36868
  9.5 0.7 copy-start.8

commit v3 on v2

--- a/solution.py
+++ b/solution.py
@@ -182,7 +182,7 @@
     e0, e1 = r1 + r3, i3 - i1
     o0 = (r1 - i1 - r3 - i3) * HALF
     o1 = (r3 - i3 - r1 - i1) * HALF
-    return [p0 + e0, m0 + o0, p1 + e1, m1 + o1, p0 - e0, m0 - o0, p1 - e1, m1 - o1]
+    return (p0, m0, p1, m1), (e0, o0, e1, o1)
 
 
 def spread(tiles, lane):
@@ -201,12 +201,13 @@
 
 def kernel(
     part_hbm, wedge_hbm, levels, ft_hbm, it_hbm, xt_hbm, tw_hbm, pick_hbm, lane_hbm,
-    out,
+    out_even, out_odd,
     part, wedge, ft, it, xt, tw, pick, lanet,
-    relay, side, final, cross,
+    relay, side, final, cross, wide, total, relay2, side2, final2,
     folded0, folded1, send, held, xr, xi, level1, level2, own_ids, mir_ids, mir_in, spec_in, back, got, mid,
     load_sem, table_sem, relay_s, relay_r, side_s, side_r, final_s, final_r, cross_s, cross_r,
-    first_s, first_r, second_s, second_r, wedge_s, wedge_r, met,
+    first_s, first_r, second_s, second_r, wedge_s, wedge_r,
+    wide_s, wide_r, relay2_s, relay2_r, side2_s, side2_r, final2_s, final2_r, met,
 ):
     shot = lax.axis_index("shot")
     lat = lax.axis_index("lat")
@@ -331,11 +332,14 @@
     def fold(c):
         for h in range(2):
             pltpu.make_async_copy(cross.at[c, h], cross.at[c, h], cross_r.at[c, h]).wait()
-        top, low = pl.ds(c * CROWS, CROWS), pl.ds(ROWS + c * CROWS, CROWS)
         u = []
         for k in range(8):
             cols = pl.ds(256 * k, 256)
             u.append(cross[c, 0, :, cols].astype(F32) + cross[c, 1, :, cols].astype(F32))
+        keep(c, u)
+
+    def keep(c, u):
+        top, low = pl.ds(c * CROWS, CROWS), pl.ds(ROWS + c * CROWS, CROWS)
         zero, four, one, two, three = real_eight(u)
         zero, four = zero.astype(BF16), four.astype(BF16)
         blank = jnp.zeros((CROWS, 512), BF16)
@@ -351,6 +355,77 @@
             folded1[s, top, 256:512] = neg
             folded1[s, low, 0:256] = im
             folded1[s, low, 256:512] = re
+
+    halves = (pl.ds(0, N // 2), pl.ds(N // 2, N // 2))
+    y_order = (y_far, y_up, y_down, y)
+
+    def wide_copy(c, j, h):
+        return copy_to(
+            slab(2 * y_order[j] + h, c), wide.at[c, xh, j], wide_s.at[c, j, h], wide_r.at[c, j, xh],
+            2 * y + h, flip,
+        )
+
+    def wide_prepare(c):
+        loads[c].wait()
+        for q in range(8):
+            part[0, q, rows(c), :] = pair(q, c).astype(BF16)
+
+    def wide_launch(c):
+        for j in range(4):
+            for h in range(2):
+                wide_copy(c, j, h).start()
+
+    def wide_sum(c, j):
+        for h in range(2):
+            pltpu.make_async_copy(wide.at[c, h, j], wide.at[c, h, j], wide_r.at[c, j, h]).wait()
+        return wide[c, 0, j].astype(F32) + wide[c, 1, j].astype(F32)
+
+    def half_copy(c, k, j, half, target, s_sem, r_sem):
+        return copy_to(
+            total.at[c, j, :, halves[half]], target.at[c, k], s_sem.at[c, k], r_sem.at[c, k],
+            up if k == 0 else down, lat,
+        )
+
+    def relay2_copy(c, k):
+        return half_copy(c, k, 0, k, relay2, relay2_s, relay2_r)
+
+    def side2_copy(c, k):
+        return half_copy(c, k, 1 + k, 1 - k, side2, side2_s, side2_r)
+
+    def final2_copy(c, k):
+        return half_copy(c, k, 1 + k, k, final2, final2_s, final2_r)
+
+    def wide_relay(c):
+        total[c, 0] = wide_sum(c, 0).astype(BF16)
+        for k in range(2):
+            relay2_copy(c, k).start()
+
+    def wide_side(c):
+        for k in range(2):
+            total[c, 1 + k] = wide_sum(c, 1 + k).astype(BF16)
+            side2_copy(c, k).start()
+
+    def wide_final(c):
+        for k in range(2):
+            relay2_copy(c, k).wait_recv()
+            both = wide[c, 0, 1 + k, :, halves[k]].astype(F32) + wide[c, 1, 1 + k, :, halves[k]].astype(F32)
+            total[c, 1 + k, :, halves[k]] = (both + relay2[c, k].astype(F32)).astype(BF16)
+            final2_copy(c, k).start()
+
+    def wide_fold(c):
+        mine = wide_sum(c, 3)
+        for k in range(2):
+            side2_copy(c, k).wait_recv()
+            final2_copy(c, k).wait_recv()
+        u = []
+        for k in range(8):
+            half, cols = k // 4, pl.ds(256 * (k % 4), 256)
+            u.append(
+                mine[:, 256 * k : 256 * k + 256]
+                + final2[c, half, :, cols].astype(F32)
+                + side2[c, 1 - half, :, cols].astype(F32)
+            )
+        keep(c, u)
 
     def first_copy(dest):
         return copy_to(send.at[dest], held.at[flip], first_s, first_r, shot, dest)
@@ -438,34 +513,37 @@
             level2[kk, 32:40, :] = look_up(spec_mir[0:8])
 
     def stack():
-        prepare(0)
+        wide_prepare(0)
         pl.semaphore_wait(barrier, len(bits) + 3)
-        launch(0)
+        wide_launch(0)
+        begin(2)
         meet(0)
-        begin(1)
+        wide_prepare(1)
+        wide_launch(1)
         meet(1)
-        forward(0)
+        forward(2)
+        wide_relay(0)
+        begin(3)
+        wide_side(0)
         meet(2)
+        across(2)
+        forward(3)
+        meet(3)
+        wide_final(0)
         wedges_out()
-        meet(3)
-        begin(2)
-        forward(1)
         meet(4)
-        across(0)
-        begin(3)
+        wide_relay(1)
+        across(3)
+        wide_fold(0)
         meet(5)
         wedges_go()
-        forward(2)
-        across(1)
-        fold(0)
-        forward(3)
-        across(2)
-        fold(1)
+        wide_side(1)
+        wide_final(1)
+        fold(2)
         wedges_in()
-        across(3)
-        fold(2)
         for k in range(3, 7):
             tables[k].wait()
+        wide_fold(1)
         fold(3)
 
     def columns():
@@ -564,17 +642,25 @@
         def _(g):
             at = pl.ds(pl.multiple_of(8 * g, 8), 8)
             parts = [(mid[s, at, 0:256], mid[s, at, 256:512]) for s in range(4)]
-            values = real_eight_back(parts[0][0], parts[0][1], parts[1], parts[2], parts[3])
-            for k in range(8):
-                out[0, at, 256 * k : 256 * k + 256] = values[k]
+            even, odd = real_eight_back(parts[0][0], parts[0][1], parts[1], parts[2], parts[3])
+            for k in range(4):
+                out_even[0, at, 256 * k : 256 * k + 256] = even[k]
+                out_odd[0, at, 256 * k : 256 * k + 256] = odd[k]
 
     def drain():
-        for c in range(CHUNKS):
+        for c in range(2, CHUNKS):
             for k in range(2):
                 relay_copy(c, k).wait_send()
                 side_copy(c, k).wait_send()
                 final_copy(c, k).wait_send()
                 cross_copy(c, k).wait_send()
+        for c in range(2):
+            for k in range(2):
+                relay2_copy(c, k).wait_send()
+                side2_copy(c, k).wait_send()
+                final2_copy(c, k).wait_send()
+                for j in range(4):
+                    wide_copy(c, j, k).wait_send()
         sent = send.at[pl.ds(0, LAT - 1)]
         pltpu.make_async_copy(sent, sent, first_s).wait()
         sent = back.at[pl.ds(0, LAT - 1)]
@@ -606,11 +692,11 @@
     anywhere = pl.BlockSpec(memory_space=pltpu.HBM)
     vmem, dma = pltpu.VMEM, pltpu.SemaphoreType.DMA
     two = dma((CHUNKS, 2))
-    return pl.pallas_call(
+    even, odd = pl.pallas_call(
         kernel,
-        out_shape=jax.ShapeDtypeStruct((1, ROWS, N), F32),
+        out_shape=[jax.ShapeDtypeStruct((1, ROWS, N // 2), F32)] * 2,
         in_specs=[anywhere, anywhere, pl.BlockSpec(memory_space=pltpu.SMEM)] + [anywhere] * 6,
-        out_specs=pl.BlockSpec(memory_space=pltpu.VMEM),
+        out_specs=[pl.BlockSpec(memory_space=pltpu.VMEM)] * 2,
         scratch_shapes=[
             vmem(partials.shape, BF16),
             vmem(wedges.shape, jnp.int32),
@@ -619,6 +705,11 @@
             vmem((CHUNKS, 2, CROWS, N), BF16),
             vmem((CHUNKS, 2, CROWS, N), BF16),
             vmem((CHUNKS, 2, CROWS, N), BF16),
+            vmem((2, 2, 4, CROWS, N), BF16),
+            vmem((2, 4, CROWS, N), BF16),
+            vmem((2, 2, CROWS, N // 2), BF16),
+            vmem((2, 2, CROWS, N // 2), BF16),
+            vmem((2, 2, CROWS, N // 2), BF16),
             vmem((128, 1024), BF16),
             vmem((3, 128, 512), BF16),
             vmem((LAT, 32, 128), BF16),
@@ -640,13 +731,16 @@
             dma, dma, dma, dma,
             dma((3,)),
             dma((3,)),
+            dma((2, 4, 2)), dma((2, 4, 2)),
+            dma((2, 2)), dma((2, 2)), dma((2, 2)), dma((2, 2)), dma((2, 2)), dma((2, 2)),
             pltpu.SemaphoreType.REGULAR((5,)),
         ],
         compiler_params=pltpu.CompilerParams(
-            collective_id=0, has_side_effects=True, vmem_limit_bytes=32 * 1024 * 1024
+            collective_id=0, has_side_effects=True, vmem_limit_bytes=60 * 1024 * 1024
         ),
         name="stack_threshold",
     )(partials, wedges, levels, *tables)
+    return jnp.concatenate([even + odd, even - odd], axis=-1)
 
 
 def solution(mesh):

time: 67.4 us -> 63 us (0.935)
  local copies, waits for them, and re-layouts: 10.9 us -> 0 us
  Pallas kernels: 56 us -> 61 us
  other arithmetic: 0 us -> 1.9 us
    unnamed x19 -> x0, local copies, waits for them, and re-layouts: 10.9 us -> none
    pallas_call x1, Pallas kernels: 56 us -> 61 us  [on_device(): pl.pallas_call(kernel, out_shape=[jax.ShapeDtypeStruct((1, ROWS, N // 2),...]
    add x0 -> x1, other arithmetic: none -> 1.07 us  [on_device(): return jnp.concatenate([even + odd, even - odd], axis=-1)]
    concatenate x0 -> x1, other arithmetic: none -> 0.83 us  [on_device(): return jnp.concatenate([even + odd, even - odd], axis=-1)]
where the time goes in v3:
time: 63 us; the launch traced here: 62.9 us
  Pallas kernels  61 us (97%)
  other arithmetic  1.9 us (3%)
    pallas_call x1, Pallas kernels, on_device(): pl.pallas_call(kernel, out_shape=[jax.ShapeDtypeStruct((1, ROWS, N // 2),...  61 us

profile of v3, /device:TPU:1, one launch (start us, length us, event | category | flops | bytes accessed | tf_op | source)
XLA Modules:
  0.0 62.9 jit_solution(11092199470029442896)
XLA Ops:
  0.0 61.0 %stack_threshold.1 = (f32[1,64,1024]{2,1,0:T(8,128)}, f32[1,64,1024]{2,1,0:T(8,128)}) custom-call(bf16[2,8,64,2048]{3,2,1,0:T(8,128)(2,1)} %part_hbm.1, s32[64,2048]{1,0:T(8,128)} %wedge_hbm.1, f32[16]{0:T(128)} %levels.1, bf16[256,2560]{1,0:T(8,128)(2,1)} %constant.12.clone.ft_hbm, bf16[2048,512]{1,0:T(8,128)(2,1)} %constant.13.clone.it_hbm, ...), custom_call_target="tpu_custom_call" | custom-call | tf_op jit(solution)/shard_map/stack_threshold/pallas_call | solution.py:695
  61.0 1.1 %fusion = (f32[1,64,1024]{2,1,0:T(8,128)S(1)}, f32[1,64,1024]{2,1,0:T(8,128)S(1)}) fusion(f32[1,64,1024]{2,1,0:T(8,128)} %get-tuple-element.7, f32[1,64,1024]{2,1,0:T(8,128)} %get-tuple-element.8), kind=kLoop, calls=%fused_computation.1 | loop fusion | flops 131072 | bytes 1048576 | tf_op jit(solution)/shard_map/add | solution.py:743
  62.1 0.8 %pad_maximum_fusion = f32[1,64,2048]{2,1,0:T(8,128)} fusion(f32[1,64,1024]{2,1,0:T(8,128)S(1)} %get-tuple-element.10, f32[1,64,1024]{2,1,0:T(8,128)S(1)} %get-tuple-element.9), kind=kLoop, calls=%fused_computation | loop fusion | flops 131072 | bytes 1048576 | tf_op jit(solution)/shard_map/concatenate | solution.py:743

commit v4 on v3

--- a/solution.py
+++ b/solution.py
@@ -65,7 +65,7 @@
 def inverse_tables():
     ky = owned()
     y2 = np.arange(256)
-    scale = 1.0 / math.sqrt(N)
+    scale = 2.0 / math.sqrt(N)
     parts = []
     for s in range(4):
         rows = ky[:, 8 * s : 8 * s + 8].reshape(-1)
@@ -201,13 +201,13 @@
 
 def kernel(
     part_hbm, wedge_hbm, levels, ft_hbm, it_hbm, xt_hbm, tw_hbm, pick_hbm, lane_hbm,
-    out_even, out_odd,
+    out,
     part, wedge, ft, it, xt, tw, pick, lanet,
     relay, side, final, cross, wide, total, relay2, side2, final2,
     folded0, folded1, send, held, xr, xi, level1, level2, own_ids, mir_ids, mir_in, spec_in, back, got, mid,
     load_sem, table_sem, relay_s, relay_r, side_s, side_r, final_s, final_r, cross_s, cross_r,
     first_s, first_r, second_s, second_r, wedge_s, wedge_r,
-    wide_s, wide_r, relay2_s, relay2_r, side2_s, side2_r, final2_s, final2_r, met,
+    wide_s, wide_r, relay2_s, relay2_r, side2_s, side2_r, final2_s, final2_r,
 ):
     shot = lax.axis_index("shot")
     lat = lax.axis_index("lat")
@@ -235,7 +235,7 @@
              (xt_hbm, xt), (tw_hbm, tw), (it_hbm, it)]
         )
     ]
-    for c in range(1, CHUNKS):
+    for c in (2, 1, 3):
         loads[c].start()
     for copy in tables:
         copy.start()
@@ -245,23 +245,13 @@
     def greet(s, l):
         pl.semaphore_signal(barrier, inc=1, device_id=(s, l), device_id_type=MESH)
 
-    def neighbour(bit):
-        return lat + bit - 2 * bit * ((lat // bit) % 2)
-
-    bits = (1, 2, 4, 8, 16)
-    for bit in bits:
-        greet(shot, neighbour(bit))
+    @pl.loop(1, LAT)
+    def _(k):
+        greet(shot, (lat + k) % LAT)
+
     greet(up, lat)
     greet(down, lat)
     greet(other, flip)
-
-    def meet(k):
-        if k > 0:
-            pl.semaphore_wait(met.at[k - 1], 1)
-        if k < len(bits):
-            pl.semaphore_signal(
-                met.at[k], inc=1, device_id=(shot, neighbour(bits[k])), device_id_type=MESH
-            )
 
     def copy_to(src, dst, s_sem, r_sem, s, l):
         return pltpu.make_async_remote_copy(
@@ -514,36 +504,30 @@
 
     def stack():
         wide_prepare(0)
-        pl.semaphore_wait(barrier, len(bits) + 3)
+        pl.semaphore_wait(barrier, LAT + 2)
         wide_launch(0)
         begin(2)
-        meet(0)
         wide_prepare(1)
         wide_launch(1)
-        meet(1)
+        begin(3)
+        wedges_out()
+        wedges_go()
         forward(2)
+        forward(3)
         wide_relay(0)
-        begin(3)
         wide_side(0)
-        meet(2)
         across(2)
-        forward(3)
-        meet(3)
+        across(3)
         wide_final(0)
-        wedges_out()
-        meet(4)
         wide_relay(1)
-        across(3)
-        wide_fold(0)
-        meet(5)
-        wedges_go()
         wide_side(1)
         wide_final(1)
-        fold(2)
+        wide_fold(0)
         wedges_in()
         for k in range(3, 7):
             tables[k].wait()
         wide_fold(1)
+        fold(2)
         fold(3)
 
     def columns():
@@ -644,8 +628,8 @@
             parts = [(mid[s, at, 0:256], mid[s, at, 256:512]) for s in range(4)]
             even, odd = real_eight_back(parts[0][0], parts[0][1], parts[1], parts[2], parts[3])
             for k in range(4):
-                out_even[0, at, 256 * k : 256 * k + 256] = even[k]
-                out_odd[0, at, 256 * k : 256 * k + 256] = odd[k]
+                out[0, at, 256 * k : 256 * k + 256] = even[k] + odd[k]
+                out[0, at, 1024 + 256 * k : 1280 + 256 * k] = even[k] - odd[k]
 
     def drain():
         for c in range(2, CHUNKS):
@@ -692,11 +676,11 @@
     anywhere = pl.BlockSpec(memory_space=pltpu.HBM)
     vmem, dma = pltpu.VMEM, pltpu.SemaphoreType.DMA
     two = dma((CHUNKS, 2))
-    even, odd = pl.pallas_call(
+    doubled = pl.pallas_call(
         kernel,
-        out_shape=[jax.ShapeDtypeStruct((1, ROWS, N // 2), F32)] * 2,
+        out_shape=jax.ShapeDtypeStruct((1, ROWS, N), F32),
         in_specs=[anywhere, anywhere, pl.BlockSpec(memory_space=pltpu.SMEM)] + [anywhere] * 6,
-        out_specs=[pl.BlockSpec(memory_space=pltpu.VMEM)] * 2,
+        out_specs=pl.BlockSpec(memory_space=pltpu.VMEM),
         scratch_shapes=[
             vmem(partials.shape, BF16),
             vmem(wedges.shape, jnp.int32),
@@ -733,14 +717,13 @@
             dma((3,)),
             dma((2, 4, 2)), dma((2, 4, 2)),
             dma((2, 2)), dma((2, 2)), dma((2, 2)), dma((2, 2)), dma((2, 2)), dma((2, 2)),
-            pltpu.SemaphoreType.REGULAR((5,)),
         ],
         compiler_params=pltpu.CompilerParams(
             collective_id=0, has_side_effects=True, vmem_limit_bytes=60 * 1024 * 1024
         ),
         name="stack_threshold",
     )(partials, wedges, levels, *tables)
-    return jnp.concatenate([even + odd, even - odd], axis=-1)
+    return doubled * 0.5
 
 
 def solution(mesh):

time: 63 us -> 52.8 us (0.84)
  Pallas kernels: 61 us -> 50.7 us
    pallas_call x1, Pallas kernels: 61 us -> 50.7 us  [on_device(): pl.pallas_call(kernel, out_shape=jax.ShapeDtypeStruct((1, ROWS, N), F32),...]
    mul x0 -> x1, other arithmetic: none -> 1.87 us  [on_device(): return doubled * 0.5]
    add x1 -> x0, other arithmetic: 1.07 us -> none  [on_device(): return jnp.concatenate([even + odd, even - odd], axis=-1)]
    concatenate x1 -> x0, other arithmetic: 0.83 us -> none  [on_device(): return jnp.concatenate([even + odd, even - odd], axis=-1)]
where the time goes in v4:
time: 52.8 us; the launch traced here: 52.6 us
  Pallas kernels  50.7 us (96%)
  other arithmetic  1.87 us (4%)
    pallas_call x1, Pallas kernels, on_device(): pl.pallas_call(kernel, out_shape=jax.ShapeDtypeStruct((1, ROWS, N), F32),...  50.7 us
    mul x1, other arithmetic, on_device(): return doubled * 0.5  1.87 us

profile of v4, /device:TPU:1, one launch (start us, length us, event | category | flops | bytes accessed | tf_op | source)
XLA Modules:
  0.0 52.6 jit_solution(17075020413102541953)
XLA Ops:
  0.0 50.7 %stack_threshold.1 = f32[1,64,2048]{2,1,0:T(8,128)} custom-call(bf16[2,8,64,2048]{3,2,1,0:T(8,128)(2,1)} %part_hbm.1, s32[64,2048]{1,0:T(8,128)} %wedge_hbm.1, f32[16]{0:T(128)} %levels.1, bf16[256,2560]{1,0:T(8,128)(2,1)} %constant.14.clone.ft_hbm, bf16[2048,512]{1,0:T(8,128)(2,1)} %constant.15.clone.it_hbm, bf16[512,256]{1,0:T(8,128)(2,1)} %constant.16.clone.xt_hbm, ...), custom_call_target="tpu_custom_call" | custom-call | tf_op jit(solution)/shard_map/stack_threshold/pallas_call | solution.py:679
  50.8 1.9 %broadcast_multiply_fusion = f32[1,64,2048]{2,1,0:T(8,128)} fusion(f32[1,64,2048]{2,1,0:T(8,128)} %stack_threshold.1), kind=kLoop, calls=%fused_computation | loop fusion | flops 131072 | bytes 1048576 | tf_op jit(solution)/shard_map/mul | solution.py:726

commit v5 on v4

--- a/solution.py
+++ b/solution.py
@@ -245,13 +245,14 @@
     def greet(s, l):
         pl.semaphore_signal(barrier, inc=1, device_id=(s, l), device_id_type=MESH)
 
+    greet(up, lat)
+    greet(down, lat)
+    greet(other, flip)
+    greet(other, LAT - 1 - lat)
+
     @pl.loop(1, LAT)
     def _(k):
         greet(shot, (lat + k) % LAT)
-
-    greet(up, lat)
-    greet(down, lat)
-    greet(other, flip)
 
     def copy_to(src, dst, s_sem, r_sem, s, l):
         return pltpu.make_async_remote_copy(
@@ -431,14 +432,16 @@
     partner = LAT - 1 - lat
     corner = jnp.where(lat == 0, 16, LAT - lat)
 
-    def mirror_copy():
+    def mirror_copy(k):
+        some = pl.ds(8 * k, 8)
         return copy_to(
-            mir_ids.at[:, pl.ds(0, 32), :], mir_in, wedge_s.at[0], wedge_r.at[0], shot, partner
+            mir_ids.at[some, pl.ds(0, 32), :], mir_in.at[some], wedge_s.at[2 + k], wedge_r.at[2 + k],
+            shot if k == 0 else other, partner,
         )
 
     def corner_copy(k):
         src = (own_ids if k == 0 else mir_ids).at[:, pl.ds(32, 16), :]
-        return copy_to(src, spec_in.at[k], wedge_s.at[1 + k], wedge_r.at[1 + k], shot, corner)
+        return copy_to(src, spec_in.at[k], wedge_s.at[k], wedge_r.at[k], shot, corner)
 
     def wedges_out():
         for k in range(3):
@@ -466,7 +469,8 @@
             mir_ids[t] = tile.astype(BF16)
 
     def wedges_go():
-        mirror_copy().start()
+        for k in range(2):
+            mirror_copy(k).start()
 
         @pl.when(lat < 16)
         def _():
@@ -480,7 +484,8 @@
         return found
 
     def wedges_in():
-        mirror_copy().wait_recv()
+        for k in range(2):
+            mirror_copy(k).wait_recv()
 
         @pl.when(lat >= 16)
         def _():
@@ -504,7 +509,7 @@
 
     def stack():
         wide_prepare(0)
-        pl.semaphore_wait(barrier, LAT + 2)
+        pl.semaphore_wait(barrier, LAT + 3)
         wide_launch(0)
         begin(2)
         wide_prepare(1)
@@ -649,7 +654,8 @@
         pltpu.make_async_copy(sent, sent, first_s).wait()
         sent = back.at[pl.ds(0, LAT - 1)]
         pltpu.make_async_copy(sent, sent, second_s).wait()
-        mirror_copy().wait_send()
+        for k in range(2):
+            mirror_copy(k).wait_send()
 
         @pl.when(lat < 16)
         def _():
@@ -713,8 +719,8 @@
             dma((7,)),
             two, two, two, two, two, two, two, two,
             dma, dma, dma, dma,
-            dma((3,)),
-            dma((3,)),
+            dma((4,)),
+            dma((4,)),
             dma((2, 4, 2)), dma((2, 4, 2)),
             dma((2, 2)), dma((2, 2)), dma((2, 2)), dma((2, 2)), dma((2, 2)), dma((2, 2)),
         ],

time: 52.8 us -> 54.2 us (1.027)
  Pallas kernels: 50.7 us -> 52.2 us
    pallas_call x1, Pallas kernels: 50.7 us -> 52.2 us  [on_device(): pl.pallas_call(kernel, out_shape=jax.ShapeDtypeStruct((1, ROWS, N), F32),...]
where the time goes in v5:
time: 54.2 us; the launch traced here: 54 us
  Pallas kernels  52.2 us (96%)
  other arithmetic  1.87 us (3%)
    pallas_call x1, Pallas kernels, on_device(): pl.pallas_call(kernel, out_shape=jax.ShapeDtypeStruct((1, ROWS, N), F32),...  52.2 us
    mul x1, other arithmetic, on_device(): return doubled * 0.5  1.87 us

profile of v5, /device:TPU:1, one launch (start us, length us, event | category | flops | bytes accessed | tf_op | source)
XLA Modules:
  0.0 54.0 jit_solution(12708178448817958220)
XLA Ops:
  0.0 52.2 %stack_threshold.1 = f32[1,64,2048]{2,1,0:T(8,128)} custom-call(bf16[2,8,64,2048]{3,2,1,0:T(8,128)(2,1)} %part_hbm.1, s32[64,2048]{1,0:T(8,128)} %wedge_hbm.1, f32[16]{0:T(128)} %levels.1, bf16[256,2560]{1,0:T(8,128)(2,1)} %constant.14.clone.ft_hbm, bf16[2048,512]{1,0:T(8,128)(2,1)} %constant.15.clone.it_hbm, bf16[512,256]{1,0:T(8,128)(2,1)} %constant.16.clone.xt_hbm, ...), custom_call_target="tpu_custom_call" | custom-call | tf_op jit(solution)/shard_map/stack_threshold/pallas_call | solution.py:685
  52.2 1.9 %broadcast_multiply_fusion = f32[1,64,2048]{2,1,0:T(8,128)} fusion(f32[1,64,2048]{2,1,0:T(8,128)} %stack_threshold.1), kind=kLoop, calls=%fused_computation | loop fusion | flops 131072 | bytes 1048576 | tf_op jit(solution)/shard_map/mul | solution.py:732

commit v6 on v5

--- a/solution.py
+++ b/solution.py
@@ -528,7 +528,6 @@
         wide_side(1)
         wide_final(1)
         wide_fold(0)
-        wedges_in()
         for k in range(3, 7):
             tables[k].wait()
         wide_fold(1)
@@ -554,6 +553,7 @@
             first_copy((lat + k) % LAT).start()
 
         held[flip] = send[lat]
+        wedges_in()
         all_but_one = held.at[pl.ds(0, LAT - 1)]
         pltpu.make_async_copy(all_but_one, all_but_one, first_r).wait()
 

time: 54.2 us -> 54.2 us (level)
  no operation moved by 1% of the time
where the time goes in v6:
time: 54.2 us; the launch traced here: 54 us
  Pallas kernels  52.1 us (96%)
  other arithmetic  1.87 us (3%)
    pallas_call x1, Pallas kernels, on_device(): pl.pallas_call(kernel, out_shape=jax.ShapeDtypeStruct((1, ROWS, N), F32),...  52.1 us
    mul x1, other arithmetic, on_device(): return doubled * 0.5  1.87 us

profile of v6, /device:TPU:1, one launch (start us, length us, event | category | flops | bytes accessed | tf_op | source)
XLA Modules:
  0.0 54.0 jit_solution(2932981516550658362)
XLA Ops:
  0.0 52.1 %stack_threshold.1 = f32[1,64,2048]{2,1,0:T(8,128)} custom-call(bf16[2,8,64,2048]{3,2,1,0:T(8,128)(2,1)} %part_hbm.1, s32[64,2048]{1,0:T(8,128)} %wedge_hbm.1, f32[16]{0:T(128)} %levels.1, bf16[256,2560]{1,0:T(8,128)(2,1)} %constant.14.clone.ft_hbm, bf16[2048,512]{1,0:T(8,128)(2,1)} %constant.15.clone.it_hbm, bf16[512,256]{1,0:T(8,128)(2,1)} %constant.16.clone.xt_hbm, ...), custom_call_target="tpu_custom_call" | custom-call | tf_op jit(solution)/shard_map/stack_threshold/pallas_call | solution.py:685
  52.1 1.9 %broadcast_multiply_fusion = f32[1,64,2048]{2,1,0:T(8,128)} fusion(f32[1,64,2048]{2,1,0:T(8,128)} %stack_threshold.1), kind=kLoop, calls=%fused_computation | loop fusion | flops 131072 | bytes 1048576 | tf_op jit(solution)/shard_map/mul | solution.py:732

commit v7 on v6

--- a/solution.py
+++ b/solution.py
@@ -356,15 +356,14 @@
             2 * y + h, flip,
         )
 
-    def wide_prepare(c):
-        loads[c].wait()
-        for q in range(8):
+    def wide_prepare(c, j):
+        for h in range(2):
+            q = 2 * y_order[j] + h
             part[0, q, rows(c), :] = pair(q, c).astype(BF16)
 
-    def wide_launch(c):
-        for j in range(4):
-            for h in range(2):
-                wide_copy(c, j, h).start()
+    def wide_launch(c, j):
+        for h in range(2):
+            wide_copy(c, j, h).start()
 
     def wide_sum(c, j):
         for h in range(2):
@@ -439,9 +438,10 @@
             shot if k == 0 else other, partner,
         )
 
-    def corner_copy(k):
-        src = (own_ids if k == 0 else mir_ids).at[:, pl.ds(32, 16), :]
-        return copy_to(src, spec_in.at[k], wedge_s.at[k], wedge_r.at[k], shot, corner)
+    def corner_copy():
+        return copy_to(
+            mir_ids.at[:, pl.ds(32, 16), :], spec_in, wedge_s.at[0], wedge_r.at[0], shot, corner
+        )
 
     def wedges_out():
         for k in range(3):
@@ -451,7 +451,8 @@
         own, mir = chosen[:48], chosen[48:]
         tall = jnp.concatenate([own[:, 128 * t : 128 * t + 128] for t in range(16)], axis=0)
         moved = jnp.dot(tall, lanet[0:128, :], preferred_element_type=F32)
-        for t, tile in enumerate(spread([moved[48 * t : 48 * t + 48] for t in range(16)], lane)):
+        own_tiles = spread([moved[48 * t : 48 * t + 48] for t in range(16)], lane)
+        for t, tile in enumerate(own_tiles):
             own_ids[t] = tile.astype(BF16)
         tall = jnp.concatenate(
             [
@@ -466,7 +467,7 @@
         )
         moved = jnp.dot(tall, lanet[128:384, :], preferred_element_type=F32)
         for t, tile in enumerate(spread([moved[48 * t : 48 * t + 48] for t in range(16)], lane)):
-            mir_ids[t] = tile.astype(BF16)
+            mir_ids[t] = jnp.concatenate([tile[:40], own_tiles[t][32:40]], axis=0).astype(BF16)
 
     def wedges_go():
         for k in range(2):
@@ -474,8 +475,7 @@
 
         @pl.when(lat < 16)
         def _():
-            for k in range(2):
-                corner_copy(k).start()
+            corner_copy().start()
 
     def look_up(ids):
         found = jnp.full(ids.shape, levels[0], F32)
@@ -489,31 +489,38 @@
 
         @pl.when(lat >= 16)
         def _():
-            for k in range(2):
-                corner_copy(k).wait_recv()
+            corner_copy().wait_recv()
 
         @pl.loop(0, 16)
         def _(kk):
             own = own_ids[kk].astype(F32)
             mir = mir_ids[kk].astype(F32)
             got_mir = mir_in[kk].astype(F32)
-            spec_own = spec_in[0, kk].astype(F32)
-            spec_mir = spec_in[1, kk].astype(F32)
+            spec = spec_in[kk].astype(F32)
+            spec_mir, spec_own = spec[0:8], spec[8:16]
             level1[kk, 0:8, :] = look_up(jnp.where(seventh & (lat >= 16), own[32:40], own[0:8]))
             level1[kk, 8:32, :] = look_up(own[8:32])
-            level1[kk, 32:40, :] = look_up(spec_own[0:8])
-            row = jnp.where(lat == 16, mir[32:40], spec_mir[0:8])
+            level1[kk, 32:40, :] = look_up(spec_own)
+            row = jnp.where(lat == 16, mir[32:40], spec_mir)
             level2[kk, 0:8, :] = look_up(jnp.where(seventh & (lat >= 16), row, got_mir[0:8]))
             level2[kk, 8:32, :] = look_up(got_mir[8:32])
-            level2[kk, 32:40, :] = look_up(spec_mir[0:8])
+            level2[kk, 32:40, :] = look_up(spec_mir)
 
     def stack():
-        wide_prepare(0)
+        loads[0].wait()
+        wide_prepare(0, 0)
         pl.semaphore_wait(barrier, LAT + 3)
-        wide_launch(0)
+        wide_launch(0, 0)
+        wide_prepare(0, 1)
+        wide_launch(0, 1)
         begin(2)
-        wide_prepare(1)
-        wide_launch(1)
+        for j in (2, 3):
+            wide_prepare(0, j)
+            wide_launch(0, j)
+        loads[1].wait()
+        for j in range(4):
+            wide_prepare(1, j)
+            wide_launch(1, j)
         begin(3)
         wedges_out()
         wedges_go()
@@ -659,8 +666,7 @@
 
         @pl.when(lat < 16)
         def _():
-            for k in range(2):
-                corner_copy(k).wait_send()
+            corner_copy().wait_send()
 
 
     stack()
@@ -711,7 +717,7 @@
             vmem((16, 48, 128), BF16),
             vmem((16, 48, 128), BF16),
             vmem((16, 32, 128), BF16),
-            vmem((2, 16, 16, 128), BF16),
+            vmem((16, 16, 128), BF16),
             vmem((LAT, 32, 128), BF16),
             vmem((LAT, 32, 128), BF16),
             vmem((4, ROWS, 512), F32),

time: 54.2 us -> 54.1 us (level)
  no operation moved by 1% of the time
where the time goes in v7:
time: 54.1 us; the launch traced here: 54 us
  Pallas kernels  52.1 us (96%)
  other arithmetic  1.87 us (3%)
    pallas_call x1, Pallas kernels, on_device(): pl.pallas_call(kernel, out_shape=jax.ShapeDtypeStruct((1, ROWS, N), F32),...  52.1 us
    mul x1, other arithmetic, on_device(): return doubled * 0.5  1.87 us

profile of v7, /device:TPU:1, one launch (start us, length us, event | category | flops | bytes accessed | tf_op | source)
XLA Modules:
  0.0 54.0 jit_solution(11294402435975729889)
XLA Ops:
  0.0 52.1 %stack_threshold.1 = f32[1,64,2048]{2,1,0:T(8,128)} custom-call(bf16[2,8,64,2048]{3,2,1,0:T(8,128)(2,1)} %part_hbm.1, s32[64,2048]{1,0:T(8,128)} %wedge_hbm.1, f32[16]{0:T(128)} %levels.1, bf16[256,2560]{1,0:T(8,128)(2,1)} %constant.14.clone.ft_hbm, bf16[2048,512]{1,0:T(8,128)(2,1)} %constant.15.clone.it_hbm, bf16[512,256]{1,0:T(8,128)(2,1)} %constant.16.clone.xt_hbm, ...), custom_call_target="tpu_custom_call" | custom-call | tf_op jit(solution)/shard_map/stack_threshold/pallas_call | solution.py:691
  52.1 1.9 %broadcast_multiply_fusion = f32[1,64,2048]{2,1,0:T(8,128)} fusion(f32[1,64,2048]{2,1,0:T(8,128)} %stack_threshold.1), kind=kLoop, calls=%fused_computation | loop fusion | flops 131072 | bytes 1048576 | tf_op jit(solution)/shard_map/mul | solution.py:738

commit v8 on v7

--- a/solution.py
+++ b/solution.py
@@ -245,14 +245,13 @@
     def greet(s, l):
         pl.semaphore_signal(barrier, inc=1, device_id=(s, l), device_id_type=MESH)
 
+    @pl.loop(1, LAT)
+    def _(k):
+        greet(shot, (lat + k) % LAT)
+
     greet(up, lat)
     greet(down, lat)
     greet(other, flip)
-    greet(other, LAT - 1 - lat)
-
-    @pl.loop(1, LAT)
-    def _(k):
-        greet(shot, (lat + k) % LAT)
 
     def copy_to(src, dst, s_sem, r_sem, s, l):
         return pltpu.make_async_remote_copy(
@@ -431,11 +430,9 @@
     partner = LAT - 1 - lat
     corner = jnp.where(lat == 0, 16, LAT - lat)
 
-    def mirror_copy(k):
-        some = pl.ds(8 * k, 8)
+    def mirror_copy():
         return copy_to(
-            mir_ids.at[some, pl.ds(0, 32), :], mir_in.at[some], wedge_s.at[2 + k], wedge_r.at[2 + k],
-            shot if k == 0 else other, partner,
+            mir_ids.at[:, pl.ds(0, 32), :], mir_in, wedge_s.at[1], wedge_r.at[1], shot, partner
         )
 
     def corner_copy():
@@ -470,8 +467,7 @@
             mir_ids[t] = jnp.concatenate([tile[:40], own_tiles[t][32:40]], axis=0).astype(BF16)
 
     def wedges_go():
-        for k in range(2):
-            mirror_copy(k).start()
+        mirror_copy().start()
 
         @pl.when(lat < 16)
         def _():
@@ -484,8 +480,7 @@
         return found
 
     def wedges_in():
-        for k in range(2):
-            mirror_copy(k).wait_recv()
+        mirror_copy().wait_recv()
 
         @pl.when(lat >= 16)
         def _():
@@ -509,7 +504,7 @@
     def stack():
         loads[0].wait()
         wide_prepare(0, 0)
-        pl.semaphore_wait(barrier, LAT + 3)
+        pl.semaphore_wait(barrier, LAT + 2)
         wide_launch(0, 0)
         wide_prepare(0, 1)
         wide_launch(0, 1)
@@ -661,8 +656,7 @@
         pltpu.make_async_copy(sent, sent, first_s).wait()
         sent = back.at[pl.ds(0, LAT - 1)]
         pltpu.make_async_copy(sent, sent, second_s).wait()
-        for k in range(2):
-            mirror_copy(k).wait_send()
+        mirror_copy().wait_send()
 
         @pl.when(lat < 16)
         def _():
@@ -725,8 +719,8 @@
             dma((7,)),
             two, two, two, two, two, two, two, two,
             dma, dma, dma, dma,
-            dma((4,)),
-            dma((4,)),
+            dma((2,)),
+            dma((2,)),
             dma((2, 4, 2)), dma((2, 4, 2)),
             dma((2, 2)), dma((2, 2)), dma((2, 2)), dma((2, 2)), dma((2, 2)), dma((2, 2)),
         ],

time: 54.1 us -> 53.8 us (level)
  no operation moved by 1% of the time
where the time goes in v8:
time: 53.8 us; the launch traced here: 53.7 us
  Pallas kernels  51.8 us (96%)
  other arithmetic  1.87 us (3%)
    pallas_call x1, Pallas kernels, on_device(): pl.pallas_call(kernel, out_shape=jax.ShapeDtypeStruct((1, ROWS, N), F32),...  51.8 us
    mul x1, other arithmetic, on_device(): return doubled * 0.5  1.87 us

profile of v8, /device:TPU:1, one launch (start us, length us, event | category | flops | bytes accessed | tf_op | source)
XLA Modules:
  0.0 53.7 jit_solution(17356095706768348579)
XLA Ops:
  0.0 51.8 %stack_threshold.1 = f32[1,64,2048]{2,1,0:T(8,128)} custom-call(bf16[2,8,64,2048]{3,2,1,0:T(8,128)(2,1)} %part_hbm.1, s32[64,2048]{1,0:T(8,128)} %wedge_hbm.1, f32[16]{0:T(128)} %levels.1, bf16[256,2560]{1,0:T(8,128)(2,1)} %constant.14.clone.ft_hbm, bf16[2048,512]{1,0:T(8,128)(2,1)} %constant.15.clone.it_hbm, bf16[512,256]{1,0:T(8,128)(2,1)} %constant.16.clone.xt_hbm, ...), custom_call_target="tpu_custom_call" | custom-call | tf_op jit(solution)/shard_map/stack_threshold/pallas_call | solution.py:685
  51.8 1.9 %broadcast_multiply_fusion = f32[1,64,2048]{2,1,0:T(8,128)} fusion(f32[1,64,2048]{2,1,0:T(8,128)} %stack_threshold.1), kind=kLoop, calls=%fused_computation | loop fusion | flops 131072 | bytes 1048576 | tf_op jit(solution)/shard_map/mul | solution.py:732

commit v9 on v4

--- a/solution.py
+++ b/solution.py
@@ -523,7 +523,6 @@
         wide_side(1)
         wide_final(1)
         wide_fold(0)
-        wedges_in()
         for k in range(3, 7):
             tables[k].wait()
         wide_fold(1)
@@ -549,6 +548,7 @@
             first_copy((lat + k) % LAT).start()
 
         held[flip] = send[lat]
+        wedges_in()
         all_but_one = held.at[pl.ds(0, LAT - 1)]
         pltpu.make_async_copy(all_but_one, all_but_one, first_r).wait()
 

time: 52.8 us -> 52.7 us (level)
  no operation moved by 1% of the time
where the time goes in v9:
time: 52.7 us; the launch traced here: 52.6 us
  Pallas kernels  50.7 us (96%)
  other arithmetic  1.87 us (4%)
    pallas_call x1, Pallas kernels, on_device(): pl.pallas_call(kernel, out_shape=jax.ShapeDtypeStruct((1, ROWS, N), F32),...  50.7 us
    mul x1, other arithmetic, on_device(): return doubled * 0.5  1.87 us

profile of v9, /device:TPU:1, one launch (start us, length us, event | category | flops | bytes accessed | tf_op | source)
XLA Modules:
  0.0 52.6 jit_solution(7759102167194958867)
XLA Ops:
  0.0 50.7 %stack_threshold.1 = f32[1,64,2048]{2,1,0:T(8,128)} custom-call(bf16[2,8,64,2048]{3,2,1,0:T(8,128)(2,1)} %part_hbm.1, s32[64,2048]{1,0:T(8,128)} %wedge_hbm.1, f32[16]{0:T(128)} %levels.1, bf16[256,2560]{1,0:T(8,128)(2,1)} %constant.14.clone.ft_hbm, bf16[2048,512]{1,0:T(8,128)(2,1)} %constant.15.clone.it_hbm, bf16[512,256]{1,0:T(8,128)(2,1)} %constant.16.clone.xt_hbm, ...), custom_call_target="tpu_custom_call" | custom-call | tf_op jit(solution)/shard_map/stack_threshold/pallas_call | solution.py:679
  50.7 1.9 %broadcast_multiply_fusion = f32[1,64,2048]{2,1,0:T(8,128)} fusion(f32[1,64,2048]{2,1,0:T(8,128)} %stack_threshold.1), kind=kLoop, calls=%fused_computation | loop fusion | flops 131072 | bytes 1048576 | tf_op jit(solution)/shard_map/mul | solution.py:726
